TPU v7x, 256 devices: a whole 4x4x8 slice. The times are simulated.
256 devices in a mesh: dp: 128 (over y, z_hi, x, core), tensor: 2 (over z_lo).
Axes of the slice: x: 4, y: 4, z: 8 (z_hi: 4, z_lo: 2; z = z_hi * 2 + z_lo), core: 2. Of those that a mesh axis runs over, the one named last changes fastest.
Arguments:
- tokens: bfloat16 [256, 197, 384], P(('dp', 'tensor')), may hold values from -6 to 6
- attn_gain: float32 [384], replicated, may hold values from 0.5 to 1.5
- attn_shift: float32 [384], replicated, may hold values from -0.625 to 0.625
- w_qkv: bfloat16 [384, 6, 192], P(None, 'tensor'), may hold values from -0.3125 to 0.3125
- qv_bias: bfloat16 [6, 128], P('tensor'), may hold values from -0.3125 to 0.3125
- w_out: bfloat16 [6, 64, 384], P('tensor'), may hold values from -2 to 2
- out_bias: bfloat16 [384], replicated, may hold values from -1.25 to 1.25
- moe_gain: float32 [384], replicated, may hold values from 0.5 to 1.5
- moe_shift: float32 [384], replicated, may hold values from -0.625 to 0.625
- router: bfloat16 [384, 3], replicated, may hold values from -0.21875 to 0.21875
- w_in: bfloat16 [3, 384, 1536], P(None, None, 'tensor'), may hold values from -0.3125 to 0.3125
- in_bias: bfloat16 [3, 1536], P(None, 'tensor'), may hold values from -1.25 to 1.25
- w_exp: bfloat16 [3, 1536, 384], P(None, 'tensor'), may hold values from -0.4375 to 0.4375
- exp_bias: bfloat16 [3, 384], replicated, may hold values from -1.25 to 1.25
- routes: int32 [256, 197, 2], P('dp'), may hold values from 0 to 2, all different within a row
- cotangent: bfloat16 [256, 197, 384], P(('dp', 'tensor')), may hold values from -6 to 6
Outputs:
- block_out: bfloat16 [256, 197, 384], P(('dp', 'tensor'))
- grad_tokens: bfloat16 [256, 197, 384], P(('dp', 'tensor'))
- grad_attn_gain: float32 [384], replicated
- grad_attn_shift: float32 [384], replicated
- grad_w_qkv: float32 [384, 6, 192], P(None, 'tensor')
- grad_qv_bias: float32 [6, 128], P('tensor')
- grad_w_out: float32 [6, 64, 384], P('tensor')
- grad_out_bias: float32 [384], replicated
- grad_moe_gain: float32 [384], replicated
- grad_moe_shift: float32 [384], replicated
- grad_router: float32 [384, 3], replicated
- grad_w_in: float32 [3, 384, 1536], P(None, None, 'tensor')
- grad_in_bias: float32 [3, 1536], P(None, 'tensor')
- grad_w_exp: float32 [3, 1536, 384], P(None, 'tensor')
- grad_exp_bias: float32 [3, 384], replicated
Inputs may be any that keep to these rules, and one draw needn't show every extreme that they name: `routes`: each token names 2 different experts.
All inputs are finite; a program needn't handle non-finite values.
Results may differ from a plain program's by a relative error of at most 0.019.
Values may be sent and summed in bfloat16 or wider, within the bound.
A program may use at most 128 MiB of HBM per device.

v0:
```python
import math

import jax
import jax.numpy as jnp
from jax import lax
from jax.sharding import PartitionSpec as P

CAP = 128


highest = lax.Precision.HIGHEST


def layer_norm(values, gain_vec, shift_vec):
    centre = values - jnp.mean(values, axis=-1, keepdims=True)
    spread = jnp.mean(centre * centre, axis=-1, keepdims=True)
    return centre * lax.rsqrt(spread + 1e-06) * gain_vec + shift_vec


def gelu_slope(values):
    return 0.5 * (1.0 + lax.erf(values * (1.0 / math.sqrt(2.0)))) + values * jnp.exp(
        -0.5 * values * values
    ) * (1.0 / math.sqrt(2.0 * math.pi))


def routing_tables(routes, capacity, experts):
    images, length, pick_count = routes.shape
    expert_ids = jnp.arange(experts, dtype=jnp.int32)
    chosen = (routes[..., None] == expert_ids).astype(jnp.int32)
    ordered = jnp.transpose(chosen, (0, 2, 1, 3)).reshape(images, pick_count * length, experts)
    earlier = jnp.cumsum(ordered, axis=1) - ordered
    slot_pos = jnp.sum(earlier * ordered, axis=-1).reshape(images, pick_count, length)
    slot_pos = jnp.transpose(slot_pos, (0, 2, 1))
    kept_mask = slot_pos < capacity
    target = jnp.where(kept_mask, routes * capacity + slot_pos, experts * capacity)
    return (chosen, kept_mask, target)


def on_device(
    tokens,
    attn_gain,
    attn_shift,
    w_qkv,
    qv_bias,
    w_out,
    out_bias,
    moe_gain,
    moe_shift,
    router,
    w_in,
    in_bias,
    w_exp,
    exp_bias,
    routes,
    cotangent,
):
    own_images, length, model_width = tokens.shape
    group_images = routes.shape[0]
    pick_count = routes.shape[2]
    experts = w_in.shape[0]
    local_heads = w_qkv.shape[1]
    head_dim = w_qkv.shape[2] // 3
    own_rows = own_images * length
    all_rows = group_images * length
    slot_count = experts * CAP
    score_scale = 1.0 / math.sqrt(head_dim)
    own_start = lax.axis_index("tensor") * own_images
    tok_flat = tokens.reshape(own_rows, model_width).astype(jnp.float32)
    normed_own, attn_norm_back = jax.vjp(layer_norm, tok_flat, attn_gain, attn_shift)
    normed_all = lax.all_gather(
        normed_own.astype(jnp.bfloat16).reshape(own_images, length, model_width),
        "tensor",
        axis=0,
        tiled=True,
    ).reshape(all_rows, model_width)
    w_qkv_flat = w_qkv.reshape(model_width, local_heads * 3 * head_dim)
    project = jnp.dot(normed_all, w_qkv_flat, preferred_element_type=jnp.float32).reshape(
        group_images, length, local_heads, 3 * head_dim
    )
    bias_float = qv_bias.astype(jnp.float32)
    queries = (project[..., :head_dim] + bias_float[:, :head_dim]).astype(jnp.bfloat16)
    key_rows = project[..., head_dim : 2 * head_dim].astype(jnp.bfloat16)
    value_rows = (project[..., 2 * head_dim :] + bias_float[:, head_dim:]).astype(jnp.bfloat16)
    scores = (
        jnp.einsum("gqhc,gkhc->ghqk", queries, key_rows, preferred_element_type=jnp.float32)
        * score_scale
    )
    row_top = jnp.max(scores, axis=-1, keepdims=True)
    weights = jnp.exp(scores - row_top)
    totals = jnp.sum(weights, axis=-1, keepdims=True)
    log_total = row_top + jnp.log(totals)
    attn_probs = weights / totals
    context = jnp.einsum(
        "ghqk,gkhc->gqhc",
        attn_probs.astype(jnp.bfloat16),
        value_rows,
        preferred_element_type=jnp.float32,
    ).astype(jnp.bfloat16)
    context_flat = context.reshape(all_rows, local_heads * head_dim)
    w_out_flat = w_out.reshape(local_heads * head_dim, model_width)
    row_part = context_flat
    attended = lax.psum_scatter(
        jnp.dot(row_part, w_out_flat, preferred_element_type=jnp.float32).astype(jnp.bfloat16),
        "tensor",
        scatter_dimension=0,
        tiled=True,
    ).astype(jnp.float32)
    hidden_in = tok_flat + attended + out_bias.astype(jnp.float32)
    moe_own, moe_norm_back = jax.vjp(layer_norm, hidden_in, moe_gain, moe_shift)
    moe_low = moe_own.astype(jnp.bfloat16)
    moe_all = lax.all_gather(
        moe_low.reshape(own_images, length, model_width), "tensor", axis=0, tiled=True
    )
    logits = jnp.dot(
        moe_all.reshape(all_rows, model_width), router, preferred_element_type=jnp.float32
    ).reshape(group_images, length, experts)
    logit_top = jnp.max(logits, axis=-1, keepdims=True)
    gate_exp = jnp.exp(logits - logit_top)
    gate_probs = gate_exp / jnp.sum(gate_exp, axis=-1, keepdims=True)
    chosen, kept_mask, target = routing_tables(routes, CAP, experts)
    chosen_float = chosen.astype(jnp.float32)
    kept_float = kept_mask.astype(jnp.float32)
    gate_pick = jnp.sum(gate_probs[:, :, None, :] * chosen_float, axis=-1)
    combine_pick = gate_pick * kept_float
    slot_ids = jnp.arange(slot_count, dtype=jnp.int32)
    onehot = (target[..., None] == slot_ids).astype(jnp.bfloat16)
    dispatch = jnp.sum(onehot, axis=2).reshape(group_images, length, experts, CAP)
    slot_in = jnp.einsum(
        "gsec,gsd->egcd", dispatch, moe_all, preferred_element_type=jnp.float32
    ).astype(jnp.bfloat16)
    pre_act = (
        jnp.einsum("egcd,edf->egcf", slot_in, w_in, preferred_element_type=jnp.float32)
        + in_bias.astype(jnp.float32)[:, None, None, :]
    )
    activated = jax.nn.gelu(pre_act, approximate=False).astype(jnp.bfloat16)
    expert_part = jnp.einsum(
        "egcf,efd->gecd", activated, w_exp, preferred_element_type=jnp.float32
    ).reshape(group_images, slot_count, model_width)
    safe_target = jnp.minimum(target, slot_count - 1).reshape(group_images, length * pick_count)
    picked = jnp.take_along_axis(expert_part, safe_target[:, :, None], axis=1).reshape(
        group_images, length, pick_count, model_width
    )
    mixed_part = jnp.sum(picked * combine_pick[..., None], axis=2).reshape(all_rows, model_width)
    moe_sum = lax.psum_scatter(
        mixed_part.astype(jnp.bfloat16), "tensor", scatter_dimension=0, tiled=True
    ).astype(jnp.float32)
    own_weight = lax.dynamic_slice_in_dim(combine_pick, own_start, own_images, 0).reshape(
        own_rows, pick_count
    )
    own_chosen = lax.dynamic_slice_in_dim(chosen_float, own_start, own_images, 0).reshape(
        own_rows, pick_count, experts
    )
    own_kept = lax.dynamic_slice_in_dim(kept_float, own_start, own_images, 0).reshape(
        own_rows, pick_count
    )
    own_gates = lax.dynamic_slice_in_dim(gate_probs, own_start, own_images, 0).reshape(
        own_rows, experts
    )
    own_share = jnp.sum(own_weight[..., None] * own_chosen, axis=1)
    exp_bias_float = exp_bias.astype(jnp.float32)
    block_out = hidden_in + moe_sum + jnp.dot(own_share, exp_bias_float, precision=highest)
    cot_own = cotangent.reshape(own_rows, model_width).astype(jnp.float32)
    cot_all = lax.all_gather(cotangent, "tensor", axis=0, tiled=True).astype(jnp.float32)
    scaled = (combine_pick[..., None] * cot_all[:, :, None, :]).astype(jnp.bfloat16)
    grad_slot = (
        jnp.einsum("gskt,gskd->gtd", onehot, scaled, preferred_element_type=jnp.float32)
        .astype(jnp.bfloat16)
        .reshape(group_images, experts, CAP, model_width)
    )
    grad_w_exp = jnp.einsum(
        "egcf,gecd->efd", activated, grad_slot, preferred_element_type=jnp.float32
    )
    grad_act = jnp.einsum("gecd,efd->egcf", grad_slot, w_exp, preferred_element_type=jnp.float32)
    grad_pre = (grad_act * gelu_slope(pre_act)).astype(jnp.bfloat16)
    grad_w_in = jnp.einsum("egcd,egcf->edf", slot_in, grad_pre, preferred_element_type=jnp.float32)
    grad_in_bias = jnp.sum(grad_pre.astype(jnp.float32), axis=(1, 2))
    grad_slot_in = jnp.einsum(
        "egcf,edf->gecd", grad_pre, w_in, preferred_element_type=jnp.float32
    ).reshape(group_images, slot_count, model_width)
    back_picked = jnp.take_along_axis(grad_slot_in, safe_target[:, :, None], axis=1).reshape(
        group_images, length, pick_count, model_width
    )
    grad_moe_part = jnp.sum(back_picked * kept_float[..., None], axis=2).reshape(
        all_rows, model_width
    )
    grad_pick_part = jnp.sum(picked * cot_all[:, :, None, :], axis=-1).reshape(all_rows, pick_count)
    grad_moe_own, grad_pick_own = (
        lax.psum_scatter(
            grad_moe_part.astype(jnp.bfloat16), "tensor", scatter_dimension=0, tiled=True
        ).astype(jnp.float32),
        lax.psum_scatter(
            grad_pick_part.astype(jnp.bfloat16), "tensor", scatter_dimension=0, tiled=True
        ).astype(jnp.float32),
    )
    cot_bias = jnp.dot(cot_own, exp_bias_float.T, precision=highest)
    pick_bias = jnp.sum(own_chosen * cot_bias[:, None, :], axis=-1)
    grad_gate_pick = (grad_pick_own + pick_bias) * own_kept
    grad_gates = jnp.sum(grad_gate_pick[..., None] * own_chosen, axis=1)
    grad_logits = own_gates * (grad_gates - jnp.sum(own_gates * grad_gates, axis=-1, keepdims=True))
    grad_router = jnp.einsum(
        "sd,se->de", moe_low.astype(jnp.float32), grad_logits, precision=highest
    )
    grad_moe_total = grad_moe_own + jnp.dot(
        grad_logits, router.astype(jnp.float32).T, precision=highest
    )
    grad_hidden_norm, grad_moe_gain, grad_moe_shift = moe_norm_back(grad_moe_total)
    grad_hidden = cot_own + grad_hidden_norm
    grad_out_bias = jnp.sum(grad_hidden, axis=0)
    grad_exp_bias = jnp.einsum("se,sd->ed", own_share, cot_own, precision=highest)
    grad_hidden_all = lax.all_gather(
        grad_hidden.astype(jnp.bfloat16).reshape(own_images, length, model_width),
        "tensor",
        axis=0,
        tiled=True,
    ).reshape(all_rows, model_width)
    grad_w_out = jnp.einsum(
        "rc,rd->cd", context_flat, grad_hidden_all, preferred_element_type=jnp.float32
    ).reshape(local_heads, head_dim, model_width)
    grad_context = (
        lax.dot_general(
            grad_hidden_all,
            w_out_flat,
            (((1,), (1,)), ((), ())),
            preferred_element_type=jnp.float32,
        )
        .astype(jnp.bfloat16)
        .reshape(group_images, length, local_heads, head_dim)
    )
    scores_again = (
        jnp.einsum("gqhc,gkhc->ghqk", queries, key_rows, preferred_element_type=jnp.float32)
        * score_scale
    )
    probs_again = jnp.exp(scores_again - log_total)
    grad_probs = jnp.einsum(
        "gqhc,gkhc->ghqk", grad_context, value_rows, preferred_element_type=jnp.float32
    )
    row_dot = jnp.sum(grad_probs * probs_again, axis=-1, keepdims=True)
    grad_raw = (probs_again * (grad_probs - row_dot) * score_scale).astype(jnp.bfloat16)
    grad_queries = jnp.einsum(
        "ghqk,gkhc->gqhc", grad_raw, key_rows, preferred_element_type=jnp.float32
    ).astype(jnp.bfloat16)
    grad_keys = jnp.einsum(
        "ghqk,gqhc->gkhc", grad_raw, queries, preferred_element_type=jnp.float32
    ).astype(jnp.bfloat16)
    grad_values = jnp.einsum(
        "ghqk,gqhc->gkhc",
        probs_again.astype(jnp.bfloat16),
        grad_context,
        preferred_element_type=jnp.float32,
    ).astype(jnp.bfloat16)
    grad_project = jnp.concatenate([grad_queries, grad_keys, grad_values], axis=-1).reshape(
        all_rows, local_heads * 3 * head_dim
    )
    grad_w_qkv = jnp.einsum(
        "rd,rc->dc", normed_all, grad_project, preferred_element_type=jnp.float32
    ).reshape(model_width, local_heads, 3 * head_dim)
    grad_qv_bias = jnp.concatenate(
        [
            jnp.sum(grad_queries.astype(jnp.float32), axis=(0, 1)),
            jnp.sum(grad_values.astype(jnp.float32), axis=(0, 1)),
        ],
        axis=-1,
    )
    row_part = grad_project
    grad_normed = lax.psum_scatter(
        lax.dot_general(
            row_part, w_qkv_flat, (((1,), (1,)), ((), ())), preferred_element_type=jnp.float32
        ).astype(jnp.bfloat16),
        "tensor",
        scatter_dimension=0,
        tiled=True,
    ).astype(jnp.float32)
    grad_tok_norm, grad_attn_gain, grad_attn_shift = attn_norm_back(grad_normed)
    grad_tokens = grad_hidden + grad_tok_norm
    grad_w_qkv, grad_qv_bias, grad_w_out, grad_w_in, grad_in_bias, grad_w_exp = lax.psum(
        (grad_w_qkv, grad_qv_bias, grad_w_out, grad_w_in, grad_in_bias, grad_w_exp), "dp"
    )
    (
        grad_attn_gain,
        grad_attn_shift,
        grad_out_bias,
        grad_moe_gain,
        grad_moe_shift,
        grad_router,
        grad_exp_bias,
    ) = lax.psum(
        (
            grad_attn_gain,
            grad_attn_shift,
            grad_out_bias,
            grad_moe_gain,
            grad_moe_shift,
            grad_router,
            grad_exp_bias,
        ),
        ("dp", "tensor"),
    )
    return (
        block_out.astype(jnp.bfloat16).reshape(own_images, length, model_width),
        grad_tokens.astype(jnp.bfloat16).reshape(own_images, length, model_width),
        grad_attn_gain,
        grad_attn_shift,
        grad_w_qkv,
        grad_qv_bias,
        grad_w_out,
        grad_out_bias,
        grad_moe_gain,
        grad_moe_shift,
        grad_router,
        grad_w_in,
        grad_in_bias,
        grad_w_exp,
        grad_exp_bias,
    )


def solution(mesh):
    placed = (
        P(("dp", "tensor"), None, None),
        P(),
        P(),
        P(None, "tensor", None),
        P("tensor", None),
        P("tensor", None, None),
        P(),
        P(),
        P(),
        P(),
        P(None, None, "tensor"),
        P(None, "tensor"),
        P(None, "tensor", None),
        P(),
        P("dp", None, None),
        P(("dp", "tensor"), None, None),
    )
    return jax.shard_map(
        on_device,
        mesh=mesh,
        in_specs=placed,
        out_specs=(
            P(("dp", "tensor"), None, None),
            P(("dp", "tensor"), None, None),
            P(),
            P(),
            P(None, "tensor", None),
            P("tensor", None),
            P("tensor", None, None),
            P(),
            P(),
            P(),
            P(),
            P(None, None, "tensor"),
            P(None, "tensor"),
            P(None, "tensor", None),
            P(),
        ),
        check_vma=False,
    )
```

profile of v0, /device:TPU:1, one launch (start us, length us, event | category | flops | bytes accessed | tf_op | source)
XLA Modules:
  0.0 1532.4 jit_solution(6939597999191063875)
XLA Ops:
  12.0 5.8 all_gather.12
  21.5 8.0 fusion
  29.6 2.5 collective-permute-start
  37.6 4.7 all_gather.14
  49.7 4.7 all-gather.2
  57.4 5.7 fusion.9
  65.0 13.3 gather_fusion
  78.3 2.5 reshape.299
  83.4 2.6 multiply_reduce_fusion.1
  89.5 2.4 convolution_bitcast_fusion.1
  92.0 2.6 convolution_bitcast_fusion
  95.5 11.0 gather_fusion.1
  109.0 6.5 fusion.139
  115.5 1.9 collective-permute-start.3
  121.8 5.4 all-gather.3
  132.2 3.1 fusion.57
  135.3 3.1 convert_reduce_fusion.4
  144.9 7.8 fusion.138
  152.7 3.4 collective-permute-start.4
  157.5 689.6 %all-reduce.12 = (f32[3,128]{1,0:T(4,128)}, f32[3,768]{1,0:T(4,128)}) all-reduce(f32[3,128]{1,0:T(4,128)S(1)} %pad_maximum_fusion.1, f32[3,768]{1,0:T(4,128)S(1)} %get-tuple-element.71), channel_id=1, replica_groups=mesh['dp'=128,'tensor'=2] {'dp'}, use_global_device_ids=true, to_apply=%region_37.39 | all-reduce | flops 2688 | bytes 21504 | tf_op jit(solution)/shard_map/psum | solution.py:275
  849.0 79.9 %all-reduce.11 = (f32[384]{0:T(512)}, f32[384]{0:T(512)}, f32[384]{0:T(512)}, f32[384]{0:T(512)}, f32[384]{0:T(512)}, /*index=5*/f32[384,3]{0,1:T(4,128)}, f32[3,384]{1,0:T(4,128)}) all-reduce(f32[384]{0:T(512)S(1)} %get-tuple-element.20, f32[384]{0:T(512)S(1)} %get-tuple-element.23, ...), channel_id=1, replica_groups=mesh['dp'=128,'tensor'=2] {'dp','tensor'}, use_global_device_ids=true, to_apply=%region_31.33 | all-reduce | flops 4224 | bytes 33792 | tf_op jit(solution)/shard_map/psum | solution.py:286
  930.2 585.5 %all-reduce.18.cloned.1.call-done = (f32[384,3,192]{0,2,1:T(8,128)}, f32[3,64,384]{2,1,0:T(8,128)}, f32[3,384,768]{2,1,0:T(8,128)}, f32[3,768,384]{2,1,0:T(8,128)}) async-done(((f32[384,3,192]{0,2,1:T(8,128)}, f32[3,64,384]{2,1,0:T(8,128)}, f32[3,384,768]{2,1,0:T(8,128)}, f32[3,768,384]{2,1,0:T(8,128)}), (f32[384,3,192]{0,2,1:T(8,128)}, f32[3,64,384]{2,1,0:T(8,128)}, f32[3,384,768]{2,1,0:T(8,128)}, ...) | async-done | bytes 8257552 | tf_op jit(solution)/shard_map/psum | solution.py:275
  1515.8 2.2 copy.191
  1518.7 4.2 copy.193
  (253 shorter events, 58.1 us)
Async XLA Ops:
  7.2 48.9 %copy-start = (bf16[3,384,768]{2,1,0:T(8,128)(2,1)S(1)}, bf16[3,384,768]{2,1,0:T(8,128)(2,1)}, u32[]{:S(2)}) copy-start(bf16[3,384,768]{2,1,0:T(8,128)(2,1)} %param.28) | copy-start | bytes 5308420
  7.2 1508.6 %all-reduce.18.cloned.1.call-start = ((), (), s32[]{:S(2)}) async-start(), calls=%async_computation | async-start | bytes 16515072 | tf_op jit(solution)/shard_map/psum | solution.py:275
  20.8 15.9 %copy-start.12 = (bf16[1,197,384]{2,1,0:T(8,128)(2,1)S(1)}, bf16[1,197,384]{2,1,0:T(8,128)(2,1)}, u32[]{:S(2)}) copy-start(bf16[1,197,384]{2,1,0:T(8,128)(2,1)} %param.33) | copy-start | bytes 453892
  20.8 16.0 %copy-start.58 = (bf16[3,384]{1,0:T(4,128)(2,1)S(1)}, bf16[3,384]{1,0:T(4,128)(2,1)}, u32[]{:S(2)}) copy-start(bf16[3,384]{1,0:T(4,128)(2,1)} %param.31) | copy-start | bytes 6916
  21.2 23.9 %copy-start.19 = (bf16[394,192]{0,1:T(8,128)(2,1)}, bf16[394,192]{0,1:T(8,128)(2,1)S(1)}, u32[]{:S(2)}) copy-start(bf16[394,192]{0,1:T(8,128)(2,1)S(1)} %reshape.252) | copy-start | bytes 453892
  21.2 21.9 %copy-start.61 = (u32[256]{0:T(256)S(1)}, u32[256]{0:T(256)}, u32[]{:S(2)}) copy-start(u32[256]{0:T(256)} %constant.158) | copy-start | bytes 3076
  21.2 23.1 %copy-start.60 = (bf16[384]{0:T(512)(128)(2,1)S(1)}, bf16[384]{0:T(512)(128)(2,1)}, u32[]{:S(2)}) copy-start(bf16[384]{0:T(512)(128)(2,1)} %param.24) | copy-start | bytes 2308
  29.6 17.6 %collective-permute-start = (bf16[11,384]{1,0:T(8,128)(2,1)S(1)}, bf16[11,384]{1,0:T(8,128)(2,1)}, u32[]{:S(2)}, u32[]{:S(2)}) collective-permute-start(bf16[11,384]{1,0:T(8,128)(2,1)S(1)} %slice.43), channel_id=1, source_target_pairs={{0,1},{2,3},{4,5},{6,7},{8,9},{10,11},{12,13},{14,15},{16,17},{18,... | collective-permute-start | bytes 25352
  32.1 15.0 copy-start.35
  35.0 12.1 copy-start.40
  35.1 12.1 copy-start.44
  36.8 11.7 copy-start.2
  107.7 12.5 copy-start.53
  107.7 12.5 copy-start.57
  115.5 3.2 collective-permute-start.3
  117.4 2.1 collective-permute-start.2
  144.1 704.3 %copy-start.39 = (f32[197]{0:T(256)S(1)}, f32[197]{0:T(256)}, u32[]{:S(2)}) copy-start(f32[197]{0:T(256)} %copy-done.38) | copy-start | bytes 2368
  144.1 704.3 %copy-start.42 = (f32[384]{0:T(512)S(1)}, f32[384]{0:T(512)}, u32[]{:S(2)}) copy-start(f32[384]{0:T(512)} %param.19) | copy-start | bytes 4612
  144.3 704.3 %copy-start.49 = (f32[197]{0:T(256)S(1)}, f32[197]{0:T(256)}, u32[]{:S(2)}) copy-start(f32[197]{0:T(256)} %copy-done.48) | copy-start | bytes 2368
  144.3 704.4 %copy-start.47 = (f32[197]{0:T(256)S(1)}, f32[197]{0:T(256)}, u32[]{:S(2)}) copy-start(f32[197]{0:T(256)} %copy-done.46) | copy-start | bytes 2368
  144.3 784.6 %copy-start.25 = (f32[197,384]{1,0:T(8,128)S(1)}, f32[197,384]{1,0:T(8,128)}, u32[]{:S(2)}) copy-start(f32[197,384]{1,0:T(8,128)} %copy-done.24) | copy-start | bytes 907780
  144.4 784.6 %copy-start.59 = (bf16[3,384]{1,0:T(4,128)(2,1)S(1)}, bf16[3,384]{1,0:T(4,128)(2,1)}, u32[]{:S(2)}) copy-start(bf16[3,384]{1,0:T(4,128)(2,1)} %param.31) | copy-start | bytes 6916
  152.7 694.3 %collective-permute-start.4 = (bf16[11,384]{1,0:T(8,128)(2,1)S(1)}, bf16[11,384]{1,0:T(8,128)(2,1)S(1)}, u32[]{:S(2)}, u32[]{:S(2)}) collective-permute-start(bf16[11,384]{1,0:T(8,128)(2,1)S(1)} %slice.47), channel_id=1, source_target_pairs={{0,1},{2,3},{4,5},{6,7},{8,9},{10,11},{12,13},{14,15},{16,17},{18,... | collective-permute-start | bytes 25352
  156.1 691.7 %collective-permute-start.1 = (bf16[11,384]{1,0:T(8,128)(2,1)S(1)}, bf16[11,384]{1,0:T(8,128)(2,1)S(1)}, u32[]{:S(2)}, u32[]{:S(2)}) collective-permute-start(bf16[11,384]{1,0:T(8,128)(2,1)S(1)} %slice.44), channel_id=1, source_target_pairs={{0,1},{2,3},{4,5},{6,7},{8,9},{10,11},{12,13},{14,15},{16,17},{18,... | collective-permute-start | bytes 25352
  (44 other events, 188.1 us)
Sparse Core Ops, SparseCore 0:
  143.0 1372.7 all-reduce.17
where the time goes:
time: 1530 us
  blocking collectives  813 us (53%)
  waiting for transfers between devices  586 us (38%)
  local copies, waits for them, and re-layouts  57.7 us (4%)
  matrix products  28.1 us (2%)
  other arithmetic  22.2 us (1%)
  between operations  15.8 us (1%)
    psum x1, blocking collectives, on_device(): lax.psum((grad_w_qkv, grad_qv_bias, grad_w_out, grad_w_in, grad_in_bias,...  690 us
    psum x1, waiting for transfers between devices, on_device(): lax.psum((grad_w_qkv, grad_qv_bias, grad_w_out, grad_w_in, grad_in_bias,...  586 us
    psum x1, blocking collectives, on_device(): lax.psum((grad_attn_gain, grad_attn_shift, grad_out_bias, grad_moe_gain,...  79.9 us
  transfers between devices with their start and end apart: 6, of which 2 were waited for; matrix products, arithmetic and copies ran while one was open for 1% of the time, Pallas kernels for 0%

commit v1 on v0

v1 whole, which is shorter than its diff:
```python
import functools
import math

import jax
import jax.numpy as jnp
from jax import lax
from jax.experimental import pallas as pl
from jax.experimental.pallas import tpu as pltpu
from jax.sharding import PartitionSpec as P

MESH = pl.DeviceIdType.MESH
RING = 4
D, SEQ, HEADS, HD, FF, EXPERTS, CAP = 384, 197, 3, 64, 768, 3, 128
ROWS = 208
QKV = 3 * HEADS * HD
TILE_ROWS = 16
LANES = 128
QKV_LANES = 640
IN_TILES = (D // TILE_ROWS) * (FF // LANES)
EXP_TILES = (FF // TILE_ROWS) * (D // LANES)
MOE_TILES = EXPERTS * (IN_TILES + EXP_TILES)
QKV_TILES = (D // TILE_ROWS) * (QKV_LANES // LANES)
OUT_TILES = (HEADS * HD // TILE_ROWS) * (D // LANES)
MOE_CHAINS = (224, 224, 224, 192)
ATTN_CHAINS = (64, 32, 32, 32)
CHAINS = MOE_CHAINS + ATTN_CHAINS
TILES = sum(CHAINS)
ORDERS = (
    ("core", "xa", "xb", "ya", "yb", "za", "zb"),
    ("core", "xb", "xa", "yb", "ya", "zb", "za"),
    ("core", "ya", "yb", "xa", "xb", "za", "zb"),
    ("core", "yb", "ya", "xb", "xa", "zb", "za"),
)
HALVINGS = 5
STEPS = 7
LANDING = sum(c // 2 + c // 4 + c // 8 + c // 16 + 3 * (c // 32) for c in CHAINS)
SMALL_ORDER = ("pair", "core", "xa", "xb", "ya", "yb", "za", "zb")
SMALL_ROWS = 24
SHARED_ROWS = 16
F32 = jnp.float32
BF16 = jnp.bfloat16
HIGHEST = lax.Precision.HIGHEST


def partners():
    me = lax.axis_index("dp")
    core = me % 2
    x = (me // 2) % RING
    z = (me // (2 * RING)) % RING
    y = me // (2 * RING * RING)

    def dp_index(y, z, x, core):
        return ((y * RING + z) * RING + x) * 2 + core

    def swap(v):
        return v + 1 - 2 * (v % 2)

    return {
        "core": ({"dp": dp_index(y, z, x, 1 - core)}, core),
        "xa": ({"dp": dp_index(y, z, swap(x), core)}, (x + 1) // 2 % 2),
        "xb": ({"dp": dp_index(y, z, RING - 1 - x, core)}, x // 2),
        "ya": ({"dp": dp_index(swap(y), z, x, core)}, (y + 1) // 2 % 2),
        "yb": ({"dp": dp_index(RING - 1 - y, z, x, core)}, y // 2),
        "za": ({"dp": dp_index(y, swap(z), x, core)}, (z + 1) // 2 % 2),
        "zb": ({"dp": dp_index(y, RING - 1 - z, x, core)}, z // 2),
        "pair": ({"tensor": 1 - lax.axis_index("tensor")}, lax.axis_index("tensor")),
    }


def dot(a, b, dims=((1,), (0,)), precision=None):
    return lax.dot_general(
        a, b, (dims, ((), ())), precision=precision, preferred_element_type=F32
    )


LAST = ((1,), (1,))
FIRST = ((0,), (0,))


def normalize(v):
    centre = v - jnp.mean(v, axis=-1, keepdims=True)
    r = lax.rsqrt(jnp.mean(centre * centre, axis=-1, keepdims=True) + 1e-06)
    return centre * r, r


def norm_back(grad, xhat, r, gain):
    g = grad * gain
    return r * (
        g
        - jnp.mean(g, axis=-1, keepdims=True)
        - xhat * jnp.mean(g * xhat, axis=-1, keepdims=True)
    )


def column_sum(v):
    return jnp.sum(v, axis=0, keepdims=True)


def add_tiles(ref, at, landing, landing_at, count):
    step = max(k for k in range(1, 17) if count % k == 0)

    @pl.loop(0, count // step)
    def _(i):
        rows = pl.ds(at + i * step, step)
        total = ref[rows].astype(F32) + landing[pl.ds(landing_at + i * step, step)].astype(F32)
        ref[rows] = total.astype(ref.dtype)


def store_tiles(ref, at, value):
    rows, lanes = value.shape
    per = rows // TILE_ROWS
    for j in range(-(-lanes // LANES)):
        part = value[:, j * LANES : min((j + 1) * LANES, lanes)]
        if part.shape[1] < LANES:
            part = jnp.concatenate(
                [part, jnp.zeros((rows, LANES - part.shape[1]), part.dtype)], axis=1
            )
        ref[at + j * per : at + (j + 1) * per] = part.astype(BF16).reshape(per, TILE_ROWS, LANES)


def block_kernel(
    tok_ref,
    cot_ref,
    vec_ref,
    w_qkv_ref,
    qkv_bias_ref,
    w_out_ref,
    w_in_ref,
    in_bias_ref,
    w_exp_ref,
    exp_bias_ref,
    route_col_ref,
    route_row_ref,
    block_ref,
    grad_tok_ref,
    sum_ref,
    small_out,
    held,
    landing,
    small_held,
    small_landing,
    normed,
    cots,
    moes,
    ghs,
    att_part,
    mix_part,
    gmoe_part,
    gate_part,
    gnorm_part,
    q_all,
    k_all,
    v_all,
    probs,
    ctx,
    gproj,
    slot_in,
    slot_cot,
    act_all,
    gpre_all,
    scaled_all,
    gslot_all,
    gback_all,
    attn_xhat,
    moe_xhat,
    hidden_ref,
    pair_send,
    pair_recv,
    send_sem,
    recv_sem,
    back_send,
    back_recv,
    small_send,
    small_recv,
):
    who = partners()
    barrier = pltpu.get_barrier_semaphore()
    for device, _ in who.values():
        pl.semaphore_signal(barrier, inc=1, device_id=device, device_id_type=MESH)

    def remote(src, dst, send, recv, name):
        copy = pltpu.make_async_remote_copy(
            src_ref=src,
            dst_ref=dst,
            send_sem=send,
            recv_sem=recv,
            device_id=who[name][0],
            device_id_type=MESH,
        )
        copy.start()
        return copy

    unsent = []

    def exchange(i, src, dst):
        copy = remote(src, dst, pair_send.at[i], pair_recv.at[i], "pair")
        unsent.append(copy)
        return copy

    spots = [0]

    class Chain:
        def __init__(self, c):
            self.c, self.order = c, ORDERS[c % len(ORDERS)]
            self.base, self.size, self.k = sum(CHAINS[:c]), CHAINS[c], 0

        def send(self):
            c, k = self.c, self.k
            name = self.order[k]
            give = self.base
            if k < HALVINGS:
                self.size //= 2
                bit = who[name][1]
                give = self.base + (1 - bit) * self.size
                self.base = self.base + bit * self.size
            self.spot = spots[0]
            spots[0] += self.size
            self.copy = remote(
                held.at[pl.ds(give, self.size)],
                landing.at[pl.ds(self.spot, self.size)],
                send_sem.at[c, k],
                recv_sem.at[c, k],
                name,
            )

        def send_back(self, k):
            self.back = k
            part = sum_ref.at[pl.ds(self.base, self.size)]
            self.copy = remote(
                part, part, back_send.at[self.c, k], back_recv.at[self.c, k], self.order[k]
            )
            unsent.append(self.copy)

        def advance(self):
            if self.k < STEPS:
                self.copy.wait_recv()
                if self.k < HALVINGS:
                    unsent.append(self.copy)
                else:
                    self.copy.wait_send()
                add_tiles(held, self.base, landing, self.spot, self.size)
                self.k += 1
                if self.k < STEPS:
                    self.send()
                    return
                step = max(k for k in range(1, 17) if self.size % k == 0)

                @pl.loop(0, self.size // step)
                def _(i):
                    rows = pl.ds(self.base + i * step, step)
                    sum_ref[rows] = held[rows]

                self.send_back(HALVINGS - 1)
            elif self.back >= 0:
                self.copy.wait_recv()
                self.base = self.base - who[self.order[self.back]][1] * self.size
                self.size = self.size * 2
                if self.back:
                    self.send_back(self.back - 1)
                else:
                    self.back = -1

    def small_step(k):
        rows = SHARED_ROWS if k == 0 else SMALL_ROWS
        copy = remote(
            small_held.at[k, pl.ds(0, rows)],
            small_landing.at[k, pl.ds(0, rows)],
            small_send.at[k],
            small_recv.at[k],
            SMALL_ORDER[k],
        )
        unsent.append(copy)
        return copy

    attn_gain, attn_shift = vec_ref[0:1], vec_ref[1:2]
    moe_gain, moe_shift, out_bias = vec_ref[2:3], vec_ref[3:4], vec_ref[4:5]

    tok = tok_ref[...].astype(F32)
    xhat, attn_r = normalize(tok)
    attn_xhat[...] = xhat
    normed[0] = (xhat * attn_gain + attn_shift).astype(BF16)
    pl.semaphore_wait(barrier, len(who))
    normed_copy = exchange(0, normed.at[0], normed.at[1])
    cot_copy = exchange(1, cot_ref, cots.at[1])
    cots[0] = cot_ref[...]

    key_mask = lax.broadcasted_iota(jnp.int32, (ROWS, ROWS), 1) < SEQ

    def project(i):
        proj = dot(normed[i], w_qkv_ref[...]) + qkv_bias_ref[...]
        for h in range(HEADS):
            at = h * 3 * HD
            q_all[i, h] = proj[:, at : at + HD].astype(BF16)
            k_all[i, h] = proj[:, at + HD : at + 2 * HD].astype(BF16)
            v_all[i, h] = proj[:, at + 2 * HD : at + 3 * HD].astype(BF16)

    def attend(i):
        total = jnp.zeros((ROWS, D), F32)
        for h in range(HEADS):
            scores = dot(q_all[i, h], k_all[i, h], LAST) * (1.0 / math.sqrt(HD))
            scores = jnp.where(key_mask, scores, -1e30)
            weights = jnp.exp(scores - jnp.max(scores, axis=-1, keepdims=True))
            p = weights / jnp.sum(weights, axis=-1, keepdims=True)
            probs[i, h] = p
            c = dot(p.astype(BF16), v_all[i, h]).astype(BF16)
            ctx[h, i] = c
            total += dot(c, w_out_ref[h * HD : (h + 1) * HD])
        return total

    tensor = lax.axis_index("tensor")
    before = (
        lax.broadcasted_iota(jnp.int32, (ROWS, ROWS), 1)
        < lax.broadcasted_iota(jnp.int32, (ROWS, ROWS), 0)
    ).astype(BF16)
    lane = lax.broadcasted_iota(jnp.int32, (ROWS, LANES), 1)
    sub = lax.broadcasted_iota(jnp.int32, (8, ROWS), 0)
    slot_lane = lax.broadcasted_iota(jnp.int32, (ROWS, CAP), 1).astype(F32)
    slot_sub = lax.broadcasted_iota(jnp.int32, (CAP, ROWS), 0).astype(F32)
    pos_col, pos_row = [], []
    for i in range(2):
        mine = tensor == i
        col = jnp.where(mine, route_col_ref[0], route_col_ref[1])
        row = jnp.where(mine, route_row_ref[0], route_row_ref[1])
        a0, a1 = col[:, 0:1] == lane, col[:, 1:2] == lane
        f0, f1 = a0.astype(F32), a1.astype(F32)
        c0 = dot(before, f0.astype(BF16))
        c1 = dot(before, f1.astype(BF16)) + column_sum(f0)
        pos_col.append(jnp.where(a0, c0, jnp.where(a1, c1, -1.0)))
        a0, a1 = row[0:1] == sub, row[1:2] == sub
        f0, f1 = a0.astype(F32), a1.astype(F32)
        c0 = dot(f0.astype(BF16), before, LAST)
        c1 = dot(f1.astype(BF16), before, LAST) + jnp.sum(f0, axis=1, keepdims=True)
        pos_row.append(jnp.where(a0, c0, jnp.where(a1, c1, -1.0)))
    kept_row = [((p >= 0.0) & (p < CAP)).astype(F32) for p in pos_row]

    def dispatch(i, e):
        return (pos_col[i][:, e : e + 1] == slot_lane).astype(F32)

    def dispatch_t(i, e):
        return (pos_row[i][e : e + 1] == slot_sub).astype(F32)

    project(0)
    normed_copy.wait_recv()
    project(1)
    att_part[0] = attend(1).astype(BF16)
    att_copy = exchange(2, att_part.at[0], att_part.at[1])
    own_part = attend(0)
    cot_copy.wait_recv()
    for i in range(2):
        for e in range(EXPERTS):
            slot_cot[e, i * CAP : (i + 1) * CAP] = dot(
                dispatch_t(i, e).astype(BF16), cots[i]
            ).astype(BF16)
    att_copy.wait_recv()
    hidden = tok + (own_part.astype(BF16).astype(F32) + att_part[1].astype(F32)) + out_bias
    hidden_ref[...] = hidden
    xhat, moe_r = normalize(hidden)
    moe_xhat[...] = xhat
    moes[0] = (xhat * moe_gain + moe_shift).astype(BF16)
    moe_copy = exchange(3, moes.at[0], moes.at[1])

    router = vec_ref[8:16].astype(BF16)
    expert_rows = sub < EXPERTS

    def gate(i):
        logits = jnp.where(expert_rows, dot(router, moes[i], LAST), -1e30)
        weights = jnp.exp(logits - jnp.max(logits, axis=0, keepdims=True))
        return weights / column_sum(weights)

    gates, slot_weight = [None, None], [[None] * EXPERTS, [None] * EXPERTS]

    def fill_slots(i):
        gates[i] = gate(i)
        for e in range(EXPERTS):
            pick = dispatch_t(i, e)
            slot_in[e, i * CAP : (i + 1) * CAP] = dot(pick.astype(BF16), moes[i]).astype(BF16)
            slot_weight[i][e] = jnp.sum(pick * gates[i][e : e + 1], axis=1, keepdims=True)

    fill_slots(0)
    moe_copy.wait_recv()
    fill_slots(1)

    gate_rows = [[None] * EXPERTS, [None] * EXPERTS]
    small_held[0] = jnp.zeros((SMALL_ROWS, D), F32)
    for e in range(EXPERTS):
        weight = jnp.concatenate([slot_weight[0][e], slot_weight[1][e]], axis=0)
        pre = dot(slot_in[e], w_in_ref[e]) + in_bias_ref[e : e + 1].astype(F32)
        half = 0.5 * (1.0 + lax.erf(pre * (1.0 / math.sqrt(2.0))))
        act_all[e] = (pre * half).astype(BF16)
        slope = half + pre * jnp.exp(-0.5 * pre * pre) * (1.0 / math.sqrt(2.0 * math.pi))
        g = slot_cot[e].astype(F32)
        gs = (g * weight).astype(BF16)
        gslot_all[e] = gs
        gpre = (dot(gs, w_exp_ref[e], LAST) * slope).astype(BF16)
        gpre_all[e] = gpre
        gback_all[e] = dot(gpre, w_in_ref[e], LAST).astype(BF16)
        slot_out = dot(act_all[e], w_exp_ref[e])
        scaled_all[e] = (slot_out * weight).astype(BF16)
        slot_gate = jnp.sum(slot_out * g, axis=1, keepdims=True)
        for i in range(2):
            gate_rows[i][e] = column_sum(
                dispatch_t(i, e) * slot_gate[i * CAP : (i + 1) * CAP]
            )

    def combine(i, ref):
        total = jnp.zeros((ROWS, D), F32)
        for e in range(EXPERTS):
            total += dot(dispatch(i, e).astype(BF16), ref[e, i * CAP : (i + 1) * CAP])
        return total

    def gate_grads(i):
        return jnp.concatenate(gate_rows[i] + [jnp.zeros((8 - EXPERTS, ROWS), F32)], axis=0)

    gmoe_part[0] = combine(1, gback_all).astype(BF16)
    gmoe_copy = exchange(4, gmoe_part.at[0], gmoe_part.at[1])
    gate_part[0] = gate_grads(1)
    gate_copy = exchange(5, gate_part.at[0], gate_part.at[1])
    mix_part[0] = combine(1, scaled_all).astype(BF16)
    mix_copy = exchange(6, mix_part.at[0], mix_part.at[1])

    for e in range(EXPERTS):
        at = e * (IN_TILES + EXP_TILES)
        store_tiles(held, at, dot(slot_in[e], gpre_all[e], FIRST))
        store_tiles(held, at + IN_TILES, dot(act_all[e], gslot_all[e], FIRST))
        bias = column_sum(gpre_all[e].astype(F32))
        for j in range(FF // D):
            small_held[0, 16 + 2 * e + j : 17 + 2 * e + j] = bias[:, j * D : (j + 1) * D]
    chains = [Chain(c) for c in range(len(CHAINS))]
    moe_chains = chains[: len(MOE_CHAINS)]
    attn_chains = chains[len(MOE_CHAINS) :]
    for chain in moe_chains:
        chain.send()

    own_gmoe = combine(0, gback_all).astype(BF16).astype(F32)
    own_mix = combine(0, scaled_all).astype(BF16).astype(F32)
    own_gate = gate_grads(0)
    cot = cot_ref[...].astype(F32)
    bias_rows = jnp.concatenate(
        [exp_bias_ref[...], jnp.zeros((8 - EXPERTS, D), BF16)], axis=0
    )
    share = gates[0] * kept_row[0]
    bias_grad = dot(bias_rows, cot_ref[...], LAST)
    gate_copy.wait_recv()
    grad_gates = (own_gate + gate_part[1] + bias_grad) * kept_row[0]
    grad_logits = gates[0] * (grad_gates - column_sum(gates[0] * grad_gates))
    small_held[0, 5:8] = dot(grad_logits, moes[0].astype(F32), precision=HIGHEST)[:EXPERTS]
    small_held[0, 8:11] = dot(share, cot, precision=HIGHEST)[:EXPERTS]
    router_back = dot(grad_logits, vec_ref[8:16], FIRST, HIGHEST)
    gmoe_copy.wait_recv()
    gmoe = own_gmoe + gmoe_part[1].astype(F32) + router_back
    grad_hidden = cot + norm_back(gmoe, moe_xhat[...], moe_r, moe_gain)
    ghs[0] = grad_hidden.astype(BF16)
    gh_copy = exchange(7, ghs.at[0], ghs.at[1])
    small_held[0, 2:3] = column_sum(grad_hidden)
    small_held[0, 3:4] = column_sum(gmoe * moe_xhat[...])
    small_held[0, 4:5] = column_sum(gmoe)
    mix_copy.wait_recv()
    block_ref[...] = (
        hidden_ref[...]
        + (own_mix + mix_part[1].astype(F32))
        + dot(share, bias_rows.astype(F32), FIRST, HIGHEST)
    ).astype(BF16)
    for chain in moe_chains:
        chain.advance()

    def attend_back(i):
        for h in range(HEADS):
            q, k, v, p = q_all[i, h], k_all[i, h], v_all[i, h], probs[i, h]
            gc = dot(ghs[i], w_out_ref[h * HD : (h + 1) * HD], LAST).astype(BF16)
            gp = dot(gc, v, LAST)
            row_dot = jnp.sum(gp * p, axis=-1, keepdims=True)
            graw = (p * (gp - row_dot) * (1.0 / math.sqrt(HD))).astype(BF16)
            at = h * 3 * HD
            gproj[i, :, at : at + HD] = dot(graw, k).astype(BF16)
            gproj[i, :, at + HD : at + 2 * HD] = dot(graw, q, FIRST).astype(BF16)
            gproj[i, :, at + 2 * HD : at + 3 * HD] = dot(p.astype(BF16), gc, FIRST).astype(BF16)

    attend_back(0)
    gh_copy.wait_recv()
    attend_back(1)
    gnorm_part[0] = dot(gproj[1], w_qkv_ref[...], LAST).astype(BF16)
    gnorm_copy = exchange(8, gnorm_part.at[0], gnorm_part.at[1])

    both = gproj[...].reshape(2 * ROWS, QKV)
    at = MOE_TILES
    store_tiles(held, at, dot(normed[...].reshape(2 * ROWS, D), both, FIRST))
    at += QKV_TILES
    gh_both = ghs[...].reshape(2 * ROWS, D)
    for h in range(HEADS):
        grad = dot(ctx[h].reshape(2 * ROWS, HD), gh_both, FIRST)
        for j in range(D // LANES):
            tiles = grad[:, j * LANES : (j + 1) * LANES].astype(BF16)
            spot = at + j * (OUT_TILES // 3) + h * (HD // TILE_ROWS)
            held[spot : spot + HD // TILE_ROWS] = tiles.reshape(HD // TILE_ROWS, TILE_ROWS, LANES)
    at += OUT_TILES
    held[at:TILES] = jnp.zeros((TILES - at, TILE_ROWS, LANES), BF16)
    for chain in attn_chains:
        chain.send()
    bias = column_sum(both.astype(F32))
    small_held[0, 22:23] = bias[:, :D]
    small_held[0, 23:24, 0 : QKV - D] = bias[:, D:]
    for chain in moe_chains:
        chain.advance()

    own_gnorm = dot(gproj[0], w_qkv_ref[...], LAST).astype(BF16).astype(F32)
    gnorm_copy.wait_recv()
    gnorm = own_gnorm + gnorm_part[1].astype(F32)
    xhat = attn_xhat[...]
    small_held[0, 0:1] = column_sum(gnorm * xhat)
    small_held[0, 1:2] = column_sum(gnorm)
    small_copy = small_step(0)
    grad_tok_ref[...] = (grad_hidden + norm_back(gnorm, xhat, attn_r, attn_gain)).astype(BF16)

    for k in range(STEPS + HALVINGS):
        for chain in attn_chains:
            chain.advance()
        for chain in moe_chains:
            chain.advance()
        if k < len(SMALL_ORDER):
            small_copy.wait_recv()
            if k == 0:
                small_held[1, :SHARED_ROWS] = (
                    small_held[0, :SHARED_ROWS] + small_landing[0, :SHARED_ROWS]
                )
                small_held[1, SHARED_ROWS:] = small_held[0, SHARED_ROWS:]
            elif k < len(SMALL_ORDER) - 1:
                small_held[k + 1] = small_held[k] + small_landing[k]
            else:
                small_out[...] = small_held[k] + small_landing[k]
            if k < len(SMALL_ORDER) - 1:
                small_copy = small_step(k + 1)
    for copy in unsent:
        copy.wait_send()


def run_block(*args):
    def bf(*shape):
        return pltpu.VMEM(shape, BF16)

    def fl(*shape):
        return pltpu.VMEM(shape, F32)

    dma = pltpu.SemaphoreType.DMA
    count = len(CHAINS)
    slots = 2 * CAP
    return pl.pallas_call(
        block_kernel,
        out_shape=(
            jax.ShapeDtypeStruct((ROWS, D), BF16),
            jax.ShapeDtypeStruct((ROWS, D), BF16),
            jax.ShapeDtypeStruct((TILES, TILE_ROWS, LANES), BF16),
            jax.ShapeDtypeStruct((SMALL_ROWS, D), F32),
        ),
        in_specs=[pl.BlockSpec(memory_space=pltpu.VMEM)] * len(args),
        out_specs=[pl.BlockSpec(memory_space=pltpu.VMEM)] * 4,
        scratch_shapes=[
            bf(TILES, TILE_ROWS, LANES),
            bf(LANDING, TILE_ROWS, LANES),
            fl(STEPS + 1, SMALL_ROWS, D),
            fl(STEPS + 1, SMALL_ROWS, D),
            bf(2, ROWS, D),
            bf(2, ROWS, D),
            bf(2, ROWS, D),
            bf(2, ROWS, D),
            bf(2, ROWS, D),
            bf(2, ROWS, D),
            bf(2, ROWS, D),
            fl(2, 8, ROWS),
            bf(2, ROWS, D),
            bf(2, HEADS, ROWS, HD),
            bf(2, HEADS, ROWS, HD),
            bf(2, HEADS, ROWS, HD),
            fl(2, HEADS, ROWS, ROWS),
            bf(HEADS, 2, ROWS, HD),
            bf(2, ROWS, QKV),
            bf(EXPERTS, slots, D),
            bf(EXPERTS, slots, D),
            bf(EXPERTS, slots, FF),
            bf(EXPERTS, slots, FF),
            bf(EXPERTS, slots, D),
            bf(EXPERTS, slots, D),
            bf(EXPERTS, slots, D),
            fl(ROWS, D),
            fl(ROWS, D),
            fl(ROWS, D),
            dma((9,)),
            dma((9,)),
            dma((count, STEPS)),
            dma((count, STEPS)),
            dma((count, HALVINGS)),
            dma((count, HALVINGS)),
            dma((STEPS + 1,)),
            dma((STEPS + 1,)),
        ],
        compiler_params=pltpu.CompilerParams(
            collective_id=0, has_side_effects=True, vmem_limit_bytes=56 * 1024 * 1024
        ),
    )(*args)


def unpack_kernel(sum_ref, w_qkv_ref, w_out_ref, w_in_ref, w_exp_ref):
    def spread(at, rows, out, lanes):
        per = rows // TILE_ROWS
        for j in range(-(-lanes // LANES)):
            width = min(LANES, lanes - j * LANES)
            part = sum_ref[at + j * per : at + (j + 1) * per].reshape(rows, LANES)
            out[:, j * LANES : j * LANES + width] = part[:, :width].astype(F32)

    for e in range(EXPERTS):
        at = e * (IN_TILES + EXP_TILES)
        spread(at, D, w_in_ref.at[e], FF)
        spread(at + IN_TILES, FF, w_exp_ref.at[e], D)
    spread(MOE_TILES, D, w_qkv_ref, QKV)
    spread(MOE_TILES + QKV_TILES, HEADS * HD, w_out_ref, D)


def unpack(sums):
    return pl.pallas_call(
        unpack_kernel,
        out_shape=(
            jax.ShapeDtypeStruct((D, QKV), F32),
            jax.ShapeDtypeStruct((HEADS * HD, D), F32),
            jax.ShapeDtypeStruct((EXPERTS, D, FF), F32),
            jax.ShapeDtypeStruct((EXPERTS, FF, D), F32),
        ),
        in_specs=[pl.BlockSpec(memory_space=pltpu.VMEM)],
        out_specs=[pl.BlockSpec(memory_space=pltpu.VMEM)] * 4,
        compiler_params=pltpu.CompilerParams(vmem_limit_bytes=32 * 1024 * 1024),
    )(sums)


def on_device(
    tokens,
    attn_gain,
    attn_shift,
    w_qkv,
    qv_bias,
    w_out,
    out_bias,
    moe_gain,
    moe_shift,
    router,
    w_in,
    in_bias,
    w_exp,
    exp_bias,
    routes,
    cotangent,
):
    pad = ROWS - SEQ
    tok = jnp.pad(tokens[0], ((0, pad), (0, 0)))
    cot = jnp.pad(cotangent[0], ((0, pad), (0, 0)))
    zero = jnp.zeros((3, D), F32)
    vec = jnp.concatenate(
        [
            jnp.stack([attn_gain, attn_shift, moe_gain, moe_shift, out_bias.astype(F32)]),
            zero,
            router.astype(F32).T,
            jnp.zeros((5, D), F32),
        ]
    )
    qkv_bias = (
        jnp.pad(qv_bias.astype(F32).reshape(HEADS, 2, HD), ((0, 0), (0, 1), (0, 0)))[
            :, jnp.array([0, 2, 1])
        ]
    ).reshape(1, QKV)
    routes = jnp.pad(routes, ((0, 0), (0, pad), (0, 0)), constant_values=-1)
    block, grad_tok, sums, small = run_block(
        tok,
        cot,
        vec,
        w_qkv.reshape(D, QKV),
        qkv_bias,
        w_out.reshape(HEADS * HD, D),
        w_in,
        in_bias,
        w_exp,
        exp_bias,
        routes,
        jnp.transpose(routes, (0, 2, 1)),
    )
    grad_w_qkv, grad_w_out, grad_w_in, grad_w_exp = unpack(sums)
    flat_bias = small[22:24].reshape(-1)[:QKV].reshape(HEADS, 3, HD)
    return (
        block[None, :SEQ],
        grad_tok[None, :SEQ],
        small[0],
        small[1],
        grad_w_qkv.reshape(D, HEADS, 3 * HD),
        jnp.concatenate([flat_bias[:, 0], flat_bias[:, 2]], axis=-1),
        grad_w_out.reshape(HEADS, HD, D),
        small[2],
        small[3],
        small[4],
        small[5:8].T,
        grad_w_in,
        small[16:22].reshape(EXPERTS, FF),
        grad_w_exp,
        small[8:11],
    )


def solution(mesh):
    placed = (
        P(("dp", "tensor"), None, None),
        P(),
        P(),
        P(None, "tensor", None),
        P("tensor", None),
        P("tensor", None, None),
        P(),
        P(),
        P(),
        P(),
        P(None, None, "tensor"),
        P(None, "tensor"),
        P(None, "tensor", None),
        P(),
        P("dp", None, None),
        P(("dp", "tensor"), None, None),
    )
    return jax.shard_map(
        on_device,
        mesh=mesh,
        in_specs=placed,
        out_specs=(
            P(("dp", "tensor"), None, None),
            P(("dp", "tensor"), None, None),
            P(),
            P(),
            P(None, "tensor", None),
            P("tensor", None),
            P("tensor", None, None),
            P(),
            P(),
            P(),
            P(),
            P(None, None, "tensor"),
            P(None, "tensor"),
            P(None, "tensor", None),
            P(),
        ),
        check_vma=False,
    )
```

time: 1530 us -> 124 us (0.08)
  blocking collectives: 813 us -> 0 us
  waiting for transfers between devices: 586 us -> 0 us
  Pallas kernels: 0 us -> 96 us
  local copies, waits for them, and re-layouts: 57.7 us -> 24.8 us
  matrix products: 28.1 us -> 0 us
  other arithmetic: 22.2 us -> 2 us
    psum x2 -> x0, blocking collectives: 770 us -> none  [the longest x1 690 us: on_device(): lax.psum((grad_w_qkv, grad_qv_bias, grad_w_out, grad_w_in, grad_in_bias,...]
    psum x1 -> x0, waiting for transfers between devices: 586 us -> none  [on_device(): lax.psum((grad_w_qkv, grad_qv_bias, grad_w_out, grad_w_in, grad_in_bias,...]
    pallas_call x0 -> x2, Pallas kernels: none -> 96 us  [the longest x1 92.6 us: run_block(): pl.pallas_call(block_kernel, out_shape=(jax.ShapeDtypeStruct((ROWS, D), B...]
    dot_general x25 -> x0, matrix products: 27.8 us -> none  [the longest x1 3.09 us: on_device(): jnp.einsum('ghqk,gqhc->gkhc', grad_raw, queries, preferred_element_type=j...]
    gather x5 -> x2, local copies, waits for them, and re-layouts: 27 us -> 0.57 us  [on_device(): jnp.pad(qv_bias.astype(F32).reshape(HEADS, 2, HD), ((0, 0), (0, 1), (0, 0)))]
    unnamed x3 -> x0, blocking collectives: 22.3 us -> none
    all_gather x4 -> x0, blocking collectives: 20.7 us -> none  [the longest x1 5.79 us: on_device(): lax.all_gather(normed_own.astype(jnp.bfloat16).reshape(own_images, length...]
    unnamed x142 -> x3, local copies, waits for them, and re-layouts: 21.3 us -> 3 us
  transfers between devices with their start and end apart: 6 -> 0, of which waited for: 2 -> 0; matrix products, arithmetic and copies ran while one was open for 1% -> 0% of each run, Pallas kernels for 0% -> 0%
where the time goes in v1:
time: 124 us; the launch traced here: 123 us
  Pallas kernels  96 us (77%)
  local copies, waits for them, and re-layouts  24.8 us (20%)
  other arithmetic  2 us (2%)
    pallas_call x1, Pallas kernels, run_block(): pl.pallas_call(block_kernel, out_shape=(jax.ShapeDtypeStruct((ROWS, D), B...  92.6 us
    another operation x5, local copies, waits for them, and re-layouts, on_device(): jnp.stack([attn_gain, attn_shift, moe_gain, moe_shift, out_bias.astype(F3...  3.41 us
    pallas_call x1, Pallas kernels, unpack(): pl.pallas_call(unpack_kernel, out_shape=(jax.ShapeDtypeStruct((D, QKV), F...  3.37 us
    unnamed x3, local copies, waits for them, and re-layouts  3 us

profile of v1, /device:TPU:1, one launch (start us, length us, event | category | flops | bytes accessed | tf_op | source)
XLA Modules:
  0.0 123.4 jit_solution(8478065686694496544)
XLA Ops:
  0.6 0.7 stack.18
  1.3 0.7 stack.19
  2.0 0.8 reshape.57
  2.8 0.7 reshape.63
  3.5 0.7 stack.20
  4.1 0.7 stack.21
  6.1 0.7 reshape.58.qkv_bias_ref
  6.7 1.3 %pad_bitcast_fusion.route_row_ref = s32[2,2,208]{2,1,0:T(2,128)} fusion(s32[2,197,2]{1,2,0:T(2,128)} %param.31), kind=kLoop, calls=%fused_computation.15 | loop fusion | bytes 6480 | tf_op jit(solution)/shard_map/transpose | solution.py:680
  8.0 0.7 convert_bitcast_fusion
  8.7 1.2 concatenate.6.vec_ref
  9.9 1.6 %pad.18.tok_ref = bf16[208,384]{1,0:T(8,128)(2,1)} pad(bf16[197,384]{1,0:T(8,128)(2,1)} %bitcast.23, bf16[]{:T(256)} %constant.6.clone.1), padding=0_11x0_0 | pad | bytes 311042 | tf_op jit(solution)/shard_map/jit(_pad)/pad | solution.py:651
  11.5 1.6 %pad.19.cot_ref = bf16[208,384]{1,0:T(8,128)(2,1)} pad(bf16[197,384]{1,0:T(8,128)(2,1)} %bitcast.24, bf16[]{:T(256)} %constant.6.clone.1), padding=0_11x0_0 | pad | bytes 311042 | tf_op jit(solution)/shard_map/jit(_pad)/pad | solution.py:652
  13.1 0.8 copy.52
  14.0 0.7 pad.22.clone.route_col_ref
  14.7 2.0 %copy.44.w_qkv_ref = bf16[384,576]{1,0:T(8,128)(2,1)} copy(bf16[384,576]{0,1:T(8,128)(2,1)} %bitcast.22) | data formatting | bytes 884736 | tf_op jit(solution)/shard_map/reshape | solution.py:672
  16.7 92.6 %shard_map.280 = (bf16[208,384]{1,0:T(8,128)(2,1)}, bf16[208,384]{1,0:T(8,128)(2,1)}, bf16[1024,16,128]{2,1,0:T(8,128)(2,1)}, f32[24,384]{1,0:T(8,128)}) custom-call(bf16[208,384]{1,0:T(8,128)(2,1)} %pad.18.tok_ref, bf16[208,384]{1,0:T(8,128)(2,1)} %pad.19.cot_ref, f32[16,384]{1,0:T(8,128)} %concatenate.6.vec_ref, bf16[384,576]{1,0:T(8,128)(2,1)} %copy.44.w_qkv_ref, ...), custom_call_target="tpu_custom_call" | custom-call | tf_op jit(solution)/shard_map/pallas_call | solution.py:546
  109.3 1.7 %slice_bitcast_fusion = (bf16[1,197,384]{2,1,0:T(8,128)(2,1)}, bf16[1,197,384]{2,1,0:T(8,128)(2,1)}) fusion(bf16[208,384]{1,0:T(8,128)(2,1)} %get-tuple-element.24, bf16[208,384]{1,0:T(8,128)(2,1)} %get-tuple-element.23), kind=kLoop, calls=%fused_computation.1 | loop fusion | bytes 605184 | tf_op jit(solution)/shard_map/broadcast_in_dim | solution.py:686
  111.0 0.7 slice.49
  112.5 1.5 %slice_reduce_fusion = (f32[384]{0:T(512)}, f32[384]{0:T(512)}, f32[384]{0:T(512)}, f32[384]{0:T(512)}, f32[384]{0:T(512)}) fusion(f32[24,384]{1,0:T(8,128)} %get-tuple-element.25), kind=kLoop, calls=%fused_computation.10 | loop fusion | bytes 15360 | tf_op jit(solution)/shard_map/slice | solution.py:694
  114.0 0.7 slice.57
  114.7 1.3 %fusion = (f32[3,384]{1,0:T(4,128)}, f32[384,3]{0,1:T(4,128)}) fusion(f32[24,384]{1,0:T(8,128)} %get-tuple-element.25), kind=kLoop, calls=%fused_computation.16 | loop fusion | bytes 18432 | tf_op jit(solution)/shard_map/slice | solution.py:699
  116.6 2.2 %copy-done = bf16[1024,16,128]{2,1,0:T(8,128)(2,1)S(1)} copy-done((bf16[1024,16,128]{2,1,0:T(8,128)(2,1)S(1)}, bf16[1024,16,128]{2,1,0:T(8,128)(2,1)}, u32[]{:S(2)}) %copy-start) | copy-done | bytes 4194328
  118.8 3.4 %shard_map.281 = (f32[384,576]{1,0:T(8,128)S(1)}, f32[192,384]{1,0:T(8,128)}, f32[3,384,768]{2,1,0:T(8,128)}, f32[3,768,384]{2,1,0:T(8,128)}) custom-call(bf16[1024,16,128]{2,1,0:T(8,128)(2,1)S(1)} %copy-done), custom_call_target="tpu_custom_call" | custom-call | tf_op jit(solution)/shard_map/pallas_call | solution.py:618
  122.2 1.2 copy.46
  (13 shorter events, 2.6 us)
Async XLA Ops:
  116.6 2.2 %copy-start = (bf16[1024,16,128]{2,1,0:T(8,128)(2,1)S(1)}, bf16[1024,16,128]{2,1,0:T(8,128)(2,1)}, u32[]{:S(2)}) copy-start(bf16[1024,16,128]{2,1,0:T(8,128)(2,1)} %get-tuple-element.26.sum_ref) | copy-start | bytes 12582916

commit v2 on v1

--- a/solution.py
+++ b/solution.py
@@ -15,11 +15,10 @@
 QKV = 3 * HEADS * HD
 TILE_ROWS = 16
 LANES = 128
-QKV_LANES = 640
 IN_TILES = (D // TILE_ROWS) * (FF // LANES)
 EXP_TILES = (FF // TILE_ROWS) * (D // LANES)
 MOE_TILES = EXPERTS * (IN_TILES + EXP_TILES)
-QKV_TILES = (D // TILE_ROWS) * (QKV_LANES // LANES)
+QKV_TILES = (QKV // TILE_ROWS) * (D // LANES)
 OUT_TILES = (HEADS * HD // TILE_ROWS) * (D // LANES)
 MOE_CHAINS = (224, 224, 224, 192)
 ATTN_CHAINS = (64, 32, 32, 32)
@@ -120,17 +119,21 @@
 
 def block_kernel(
     tok_ref,
-    cot_ref,
-    vec_ref,
+    attn_gain_ref,
+    attn_shift_ref,
     w_qkv_ref,
-    qkv_bias_ref,
+    qv_bias_ref,
     w_out_ref,
+    out_bias_ref,
+    moe_gain_ref,
+    moe_shift_ref,
+    router_ref,
     w_in_ref,
     in_bias_ref,
     w_exp_ref,
     exp_bias_ref,
-    route_col_ref,
-    route_row_ref,
+    route_ref,
+    cot_ref,
     block_ref,
     grad_tok_ref,
     sum_ref,
@@ -164,6 +167,8 @@
     attn_xhat,
     moe_xhat,
     hidden_ref,
+    padded,
+    route_pad,
     pair_send,
     pair_recv,
     send_sem,
@@ -272,27 +277,35 @@
         unsent.append(copy)
         return copy
 
-    attn_gain, attn_shift = vec_ref[0:1], vec_ref[1:2]
-    moe_gain, moe_shift, out_bias = vec_ref[2:3], vec_ref[3:4], vec_ref[4:5]
-
-    tok = tok_ref[...].astype(F32)
+    def row_of(ref):
+        return ref[...].astype(F32).reshape(1, D)
+
+    attn_gain, attn_shift = row_of(attn_gain_ref), row_of(attn_shift_ref)
+    moe_gain, moe_shift = row_of(moe_gain_ref), row_of(moe_shift_ref)
+    out_bias = row_of(out_bias_ref)
+
+    padded[:, SEQ - 5 :] = jnp.zeros((2, ROWS - SEQ + 5, D), F32)
+    padded[0, :SEQ] = tok_ref[0].astype(F32)
+    padded[1, :SEQ] = cot_ref[0].astype(F32)
+    tok = padded[0]
     xhat, attn_r = normalize(tok)
     attn_xhat[...] = xhat
     normed[0] = (xhat * attn_gain + attn_shift).astype(BF16)
+    cots[0] = padded[1].astype(BF16)
     pl.semaphore_wait(barrier, len(who))
     normed_copy = exchange(0, normed.at[0], normed.at[1])
-    cot_copy = exchange(1, cot_ref, cots.at[1])
-    cots[0] = cot_ref[...]
+    cot_copy = exchange(1, cots.at[0], cots.at[1])
 
     key_mask = lax.broadcasted_iota(jnp.int32, (ROWS, ROWS), 1) < SEQ
 
     def project(i):
-        proj = dot(normed[i], w_qkv_ref[...]) + qkv_bias_ref[...]
+        proj = dot(normed[i], w_qkv_ref[...], LAST)
+        bias = qv_bias_ref[...].astype(F32)
         for h in range(HEADS):
             at = h * 3 * HD
-            q_all[i, h] = proj[:, at : at + HD].astype(BF16)
+            q_all[i, h] = (proj[:, at : at + HD] + bias[h : h + 1, :HD]).astype(BF16)
             k_all[i, h] = proj[:, at + HD : at + 2 * HD].astype(BF16)
-            v_all[i, h] = proj[:, at + 2 * HD : at + 3 * HD].astype(BF16)
+            v_all[i, h] = (proj[:, at + 2 * HD : at + 3 * HD] + bias[h : h + 1, HD:]).astype(BF16)
 
     def attend(i):
         total = jnp.zeros((ROWS, D), F32)
@@ -312,15 +325,21 @@
         lax.broadcasted_iota(jnp.int32, (ROWS, ROWS), 1)
         < lax.broadcasted_iota(jnp.int32, (ROWS, ROWS), 0)
     ).astype(BF16)
-    lane = lax.broadcasted_iota(jnp.int32, (ROWS, LANES), 1)
-    sub = lax.broadcasted_iota(jnp.int32, (8, ROWS), 0)
+    lane = lax.broadcasted_iota(jnp.int32, (ROWS, LANES), 1).astype(F32)
+    sub = lax.broadcasted_iota(jnp.int32, (8, ROWS), 0).astype(F32)
     slot_lane = lax.broadcasted_iota(jnp.int32, (ROWS, CAP), 1).astype(F32)
     slot_sub = lax.broadcasted_iota(jnp.int32, (CAP, ROWS), 0).astype(F32)
+    same = (
+        lax.broadcasted_iota(jnp.int32, (ROWS, ROWS), 0)
+        == lax.broadcasted_iota(jnp.int32, (ROWS, ROWS), 1)
+    ).astype(BF16)
     pos_col, pos_row = [], []
     for i in range(2):
-        mine = tensor == i
-        col = jnp.where(mine, route_col_ref[0], route_col_ref[1])
-        row = jnp.where(mine, route_row_ref[0], route_row_ref[1])
+        route_pad[i] = jnp.full((2, ROWS), -1.0, F32)
+        first, second = route_ref[0].astype(F32), route_ref[1].astype(F32)
+        route_pad[i, :, :SEQ] = jnp.where(tensor == i, first, second)
+        row = route_pad[i]
+        col = dot(same, row.astype(BF16), LAST)
         a0, a1 = col[:, 0:1] == lane, col[:, 1:2] == lane
         f0, f1 = a0.astype(F32), a1.astype(F32)
         c0 = dot(before, f0.astype(BF16))
@@ -359,7 +378,10 @@
     moes[0] = (xhat * moe_gain + moe_shift).astype(BF16)
     moe_copy = exchange(3, moes.at[0], moes.at[1])
 
-    router = vec_ref[8:16].astype(BF16)
+    router_rows = jnp.concatenate(
+        [router_ref[...].astype(F32), jnp.zeros((8 - EXPERTS, D), F32)], axis=0
+    )
+    router = router_rows.astype(BF16)
     expert_rows = sub < EXPERTS
 
     def gate(i):
@@ -434,18 +456,18 @@
     own_gmoe = combine(0, gback_all).astype(BF16).astype(F32)
     own_mix = combine(0, scaled_all).astype(BF16).astype(F32)
     own_gate = gate_grads(0)
-    cot = cot_ref[...].astype(F32)
+    cot = padded[1]
     bias_rows = jnp.concatenate(
         [exp_bias_ref[...], jnp.zeros((8 - EXPERTS, D), BF16)], axis=0
     )
     share = gates[0] * kept_row[0]
-    bias_grad = dot(bias_rows, cot_ref[...], LAST)
+    bias_grad = dot(bias_rows, cots[0], LAST)
     gate_copy.wait_recv()
     grad_gates = (own_gate + gate_part[1] + bias_grad) * kept_row[0]
     grad_logits = gates[0] * (grad_gates - column_sum(gates[0] * grad_gates))
     small_held[0, 5:8] = dot(grad_logits, moes[0].astype(F32), precision=HIGHEST)[:EXPERTS]
     small_held[0, 8:11] = dot(share, cot, precision=HIGHEST)[:EXPERTS]
-    router_back = dot(grad_logits, vec_ref[8:16], FIRST, HIGHEST)
+    router_back = dot(grad_logits, router_rows, FIRST, HIGHEST)
     gmoe_copy.wait_recv()
     gmoe = own_gmoe + gmoe_part[1].astype(F32) + router_back
     grad_hidden = cot + norm_back(gmoe, moe_xhat[...], moe_r, moe_gain)
@@ -478,12 +500,12 @@
     attend_back(0)
     gh_copy.wait_recv()
     attend_back(1)
-    gnorm_part[0] = dot(gproj[1], w_qkv_ref[...], LAST).astype(BF16)
+    gnorm_part[0] = dot(gproj[1], w_qkv_ref[...]).astype(BF16)
     gnorm_copy = exchange(8, gnorm_part.at[0], gnorm_part.at[1])
 
     both = gproj[...].reshape(2 * ROWS, QKV)
     at = MOE_TILES
-    store_tiles(held, at, dot(normed[...].reshape(2 * ROWS, D), both, FIRST))
+    store_tiles(held, at, dot(both, normed[...].reshape(2 * ROWS, D), FIRST))
     at += QKV_TILES
     gh_both = ghs[...].reshape(2 * ROWS, D)
     for h in range(HEADS):
@@ -502,7 +524,7 @@
     for chain in moe_chains:
         chain.advance()
 
-    own_gnorm = dot(gproj[0], w_qkv_ref[...], LAST).astype(BF16).astype(F32)
+    own_gnorm = dot(gproj[0], w_qkv_ref[...]).astype(BF16).astype(F32)
     gnorm_copy.wait_recv()
     gnorm = own_gnorm + gnorm_part[1].astype(F32)
     xhat = attn_xhat[...]
@@ -583,6 +605,8 @@
             fl(ROWS, D),
             fl(ROWS, D),
             fl(ROWS, D),
+            fl(2, ROWS, D),
+            fl(2, 2, ROWS),
             dma((9,)),
             dma((9,)),
             dma((count, STEPS)),
@@ -598,35 +622,116 @@
     )(*args)
 
 
-def unpack_kernel(sum_ref, w_qkv_ref, w_out_ref, w_in_ref, w_exp_ref):
-    def spread(at, rows, out, lanes):
+def unpack_kernel(
+    block_ref,
+    grad_tok_ref,
+    sum_ref,
+    small_ref,
+    block_out,
+    grad_tok_out,
+    attn_gain,
+    attn_shift,
+    w_qkv_out,
+    qv_bias,
+    w_out_out,
+    out_bias,
+    moe_gain,
+    moe_shift,
+    router,
+    w_in_out,
+    in_bias,
+    w_exp_out,
+    exp_bias,
+    sums,
+    w_qkv,
+    w_out,
+    w_in,
+    w_exp,
+    in_sem,
+    out_sem,
+):
+    pieces = []
+    for e in range(EXPERTS):
+        at = e * (IN_TILES + EXP_TILES)
+        pieces.append((at, IN_TILES, D, FF, w_in.at[e], w_in_out.at[e]))
+        pieces.append((at + IN_TILES, EXP_TILES, FF, D, w_exp.at[e], w_exp_out.at[e]))
+    at = MOE_TILES
+    pieces.append((at, QKV_TILES, QKV, D, w_qkv, w_qkv_out))
+    pieces.append((at + QKV_TILES, OUT_TILES, HEADS * HD, D, w_out, w_out_out))
+    arriving = []
+    for i, (at, tiles, *_) in enumerate(pieces):
+        rows = pl.ds(at, tiles)
+        arriving.append(pltpu.make_async_copy(sum_ref.at[rows], sums.at[rows], in_sem.at[i]))
+        arriving[-1].start()
+    block_out[0] = block_ref[:SEQ]
+    grad_tok_out[0] = grad_tok_ref[:SEQ]
+    small = small_ref[...]
+    for ref, row in zip((attn_gain, attn_shift, out_bias, moe_gain, moe_shift), range(5)):
+        ref[...] = small[row]
+    router[...] = small[5:8]
+    exp_bias[...] = small[8:11]
+    for e in range(EXPERTS):
+        for j in range(FF // D):
+            in_bias[e : e + 1, j * D : (j + 1) * D] = small[16 + 2 * e + j : 17 + 2 * e + j]
+    bias = jnp.concatenate([small[22:23], small[23:24]], axis=1)
+    for h in range(HEADS):
+        at = 3 * h * HD
+        qv_bias[h : h + 1, :HD] = bias[:, at : at + HD]
+        qv_bias[h : h + 1, HD:] = bias[:, at + 2 * HD : at + 3 * HD]
+    leaving = []
+    for i, (at, tiles, rows, lanes, held, out) in enumerate(pieces):
+        arriving[i].wait()
         per = rows // TILE_ROWS
         for j in range(-(-lanes // LANES)):
             width = min(LANES, lanes - j * LANES)
-            part = sum_ref[at + j * per : at + (j + 1) * per].reshape(rows, LANES)
-            out[:, j * LANES : j * LANES + width] = part[:, :width].astype(F32)
-
-    for e in range(EXPERTS):
-        at = e * (IN_TILES + EXP_TILES)
-        spread(at, D, w_in_ref.at[e], FF)
-        spread(at + IN_TILES, FF, w_exp_ref.at[e], D)
-    spread(MOE_TILES, D, w_qkv_ref, QKV)
-    spread(MOE_TILES + QKV_TILES, HEADS * HD, w_out_ref, D)
-
-
-def unpack(sums):
+            part = sums[at + j * per : at + (j + 1) * per].reshape(rows, LANES)
+            held[:, j * LANES : j * LANES + width] = part[:, :width].astype(F32)
+        leaving.append(pltpu.make_async_copy(held, out, out_sem.at[i]))
+        leaving[-1].start()
+    for copy in leaving:
+        copy.wait()
+
+
+def unpack(*args):
+    def out(shape, dtype=F32):
+        return jax.ShapeDtypeStruct(shape, dtype)
+
+    vmem = pl.BlockSpec(memory_space=pltpu.VMEM)
+    anywhere = pl.BlockSpec(memory_space=pl.ANY)
+    wide = (4, 6, 11, 13)
+    shapes = (
+        out((1, SEQ, D), BF16),
+        out((1, SEQ, D), BF16),
+        out((D,)),
+        out((D,)),
+        out((QKV, D)),
+        out((HEADS, 2 * HD)),
+        out((HEADS * HD, D)),
+        out((D,)),
+        out((D,)),
+        out((D,)),
+        out((EXPERTS, D)),
+        out((EXPERTS, D, FF)),
+        out((EXPERTS, FF)),
+        out((EXPERTS, FF, D)),
+        out((EXPERTS, D)),
+    )
     return pl.pallas_call(
         unpack_kernel,
-        out_shape=(
-            jax.ShapeDtypeStruct((D, QKV), F32),
-            jax.ShapeDtypeStruct((HEADS * HD, D), F32),
-            jax.ShapeDtypeStruct((EXPERTS, D, FF), F32),
-            jax.ShapeDtypeStruct((EXPERTS, FF, D), F32),
-        ),
-        in_specs=[pl.BlockSpec(memory_space=pltpu.VMEM)],
-        out_specs=[pl.BlockSpec(memory_space=pltpu.VMEM)] * 4,
-        compiler_params=pltpu.CompilerParams(vmem_limit_bytes=32 * 1024 * 1024),
-    )(sums)
+        out_shape=shapes,
+        in_specs=[vmem, vmem, anywhere, vmem],
+        out_specs=[anywhere if i in wide else vmem for i in range(len(shapes))],
+        scratch_shapes=[
+            pltpu.VMEM((TILES, TILE_ROWS, LANES), BF16),
+            pltpu.VMEM((QKV, D), F32),
+            pltpu.VMEM((HEADS * HD, D), F32),
+            pltpu.VMEM((EXPERTS, D, FF), F32),
+            pltpu.VMEM((EXPERTS, FF, D), F32),
+            pltpu.SemaphoreType.DMA((8,)),
+            pltpu.SemaphoreType.DMA((8,)),
+        ],
+        compiler_params=pltpu.CompilerParams(vmem_limit_bytes=40 * 1024 * 1024),
+    )(*args)
 
 
 def on_device(
@@ -647,57 +752,32 @@
     routes,
     cotangent,
 ):
-    pad = ROWS - SEQ
-    tok = jnp.pad(tokens[0], ((0, pad), (0, 0)))
-    cot = jnp.pad(cotangent[0], ((0, pad), (0, 0)))
-    zero = jnp.zeros((3, D), F32)
-    vec = jnp.concatenate(
-        [
-            jnp.stack([attn_gain, attn_shift, moe_gain, moe_shift, out_bias.astype(F32)]),
-            zero,
-            router.astype(F32).T,
-            jnp.zeros((5, D), F32),
-        ]
+    outs = list(
+        unpack(
+            *run_block(
+                tokens,
+                attn_gain,
+                attn_shift,
+                jnp.transpose(w_qkv, (1, 2, 0)).reshape(QKV, D),
+                qv_bias,
+                w_out.reshape(HEADS * HD, D),
+                out_bias,
+                moe_gain,
+                moe_shift,
+                router.T,
+                w_in,
+                in_bias,
+                w_exp,
+                exp_bias,
+                jnp.transpose(routes, (0, 2, 1)),
+                cotangent,
+            )
+        )
     )
-    qkv_bias = (
-        jnp.pad(qv_bias.astype(F32).reshape(HEADS, 2, HD), ((0, 0), (0, 1), (0, 0)))[
-            :, jnp.array([0, 2, 1])
-        ]
-    ).reshape(1, QKV)
-    routes = jnp.pad(routes, ((0, 0), (0, pad), (0, 0)), constant_values=-1)
-    block, grad_tok, sums, small = run_block(
-        tok,
-        cot,
-        vec,
-        w_qkv.reshape(D, QKV),
-        qkv_bias,
-        w_out.reshape(HEADS * HD, D),
-        w_in,
-        in_bias,
-        w_exp,
-        exp_bias,
-        routes,
-        jnp.transpose(routes, (0, 2, 1)),
-    )
-    grad_w_qkv, grad_w_out, grad_w_in, grad_w_exp = unpack(sums)
-    flat_bias = small[22:24].reshape(-1)[:QKV].reshape(HEADS, 3, HD)
-    return (
-        block[None, :SEQ],
-        grad_tok[None, :SEQ],
-        small[0],
-        small[1],
-        grad_w_qkv.reshape(D, HEADS, 3 * HD),
-        jnp.concatenate([flat_bias[:, 0], flat_bias[:, 2]], axis=-1),
-        grad_w_out.reshape(HEADS, HD, D),
-        small[2],
-        small[3],
-        small[4],
-        small[5:8].T,
-        grad_w_in,
-        small[16:22].reshape(EXPERTS, FF),
-        grad_w_exp,
-        small[8:11],
-    )
+    outs[4] = jnp.transpose(outs[4].reshape(HEADS, 3 * HD, D), (2, 0, 1))
+    outs[10] = outs[10].T
+    outs[6] = outs[6].reshape(HEADS, HD, D)
+    return tuple(outs)
 
 
 def solution(mesh):

time: 124 us -> 104 us (0.84)
  local copies, waits for them, and re-layouts: 24.8 us -> 4.78 us
  Pallas kernels: 96 us -> 98.1 us
  other arithmetic: 2 us -> 0 us
    slice x6 -> x0, local copies, waits for them, and re-layouts: 4.35 us -> none  [the longest x1 1.51 us: on_device(): small[4]]
    reshape x5 -> x0, local copies, waits for them, and re-layouts: 4.03 us -> none  [the longest x1 2 us: on_device(): w_qkv.reshape(D, QKV)]
    pad x3 -> x0, local copies, waits for them, and re-layouts: 3.89 us -> none  [the longest x1 1.59 us: on_device(): tok = jnp.pad(tokens[0], ((0, pad), (0, 0)))]
    another operation x5 -> x0, local copies, waits for them, and re-layouts: 3.41 us -> none  [on_device(): jnp.stack([attn_gain, attn_shift, moe_gain, moe_shift, out_bias.astype(F3...]
    pallas_call x1, Pallas kernels: 3.37 us -> 5.62 us  [unpack(): pl.pallas_call(unpack_kernel, out_shape=shapes, in_specs=[vmem, vmem, any...]
    unnamed x3 -> x8, local copies, waits for them, and re-layouts: 3 us -> 4.78 us
    broadcast_in_dim x3 -> x0, local copies, waits for them, and re-layouts: 1.74 us -> none  [the longest x1 1.73 us: on_device(): grad_tok[None, :SEQ]]
    transpose x1 -> x0, local copies, waits for them, and re-layouts: 1.28 us -> none  [on_device(): jnp.transpose(routes, (0, 2, 1))]
where the time goes in v2:
time: 104 us
  Pallas kernels  98.1 us (94%)
  local copies, waits for them, and re-layouts  4.78 us (5%)
    pallas_call x1, Pallas kernels, run_block(): pl.pallas_call(block_kernel, out_shape=(jax.ShapeDtypeStruct((ROWS, D), B...  92.5 us
    pallas_call x1, Pallas kernels, unpack(): pl.pallas_call(unpack_kernel, out_shape=shapes, in_specs=[vmem, vmem, any...  5.62 us
    unnamed x8, local copies, waits for them, and re-layouts  4.78 us

profile of v2, /device:TPU:1, one launch (start us, length us, event | category | flops | bytes accessed | tf_op | source)
XLA Modules:
  0.0 103.7 jit_solution(15612956560285561728)
XLA Ops:
  0.7 92.5 %shard_map.271 = (bf16[208,384]{1,0:T(8,128)(2,1)}, bf16[208,384]{1,0:T(8,128)(2,1)}, bf16[1024,16,128]{2,1,0:T(8,128)(2,1)}, f32[24,384]{1,0:T(8,128)}) custom-call(bf16[1,197,384]{2,1,0:T(8,128)(2,1)} %tok_ref.1, f32[384]{0:T(512)} %attn_gain_ref.1, f32[384]{0:T(512)} %attn_shift_ref.1, bf16[576,384]{1,0:T(8,128)(2,1)} %bitcast.11, ...), custom_call_target="tpu_custom_call" | custom-call | tf_op jit(solution)/shard_map/pallas_call | solution.py:568
  93.2 0.0 copy-start
  93.2 2.2 %copy-done = bf16[1024,16,128]{2,1,0:T(8,128)(2,1)S(1)} copy-done((bf16[1024,16,128]{2,1,0:T(8,128)(2,1)S(1)}, bf16[1024,16,128]{2,1,0:T(8,128)(2,1)}, u32[]{:S(2)}) %copy-start) | copy-done | bytes 4194328
  95.4 0.0 copy-start.1
  95.4 0.9 copy-done.1
  96.3 0.0 copy-start.2
  96.3 0.9 copy-done.2
  97.2 0.0 copy-start.3
  97.2 0.8 copy-done.3
  98.0 5.6 %shard_map.272 = (bf16[1,197,384]{2,1,0:T(8,128)(2,1)}, bf16[1,197,384]{2,1,0:T(8,128)(2,1)}, f32[384]{0:T(512)}, f32[384]{0:T(512)}, f32[576,384]{1,0:T(8,128)}...) custom-call(bf16[208,384]{1,0:T(8,128)(2,1)S(1)} %copy-done.1, ...), custom_call_target="tpu_custom_call" | custom-call | tf_op jit(solution)/shard_map/pallas_call | solution.py:719
Async XLA Ops:
  93.2 2.2 %copy-start = (bf16[1024,16,128]{2,1,0:T(8,128)(2,1)S(1)}, bf16[1024,16,128]{2,1,0:T(8,128)(2,1)}, u32[]{:S(2)}) copy-start(bf16[1024,16,128]{2,1,0:T(8,128)(2,1)} %get-tuple-element.36.sum_ref) | copy-start | bytes 12582916
  95.4 0.9 copy-start.1
  96.3 0.9 copy-start.2
  97.2 0.8 copy-start.3

commit v3 on v2

--- a/solution.py
+++ b/solution.py
@@ -20,50 +20,40 @@
 MOE_TILES = EXPERTS * (IN_TILES + EXP_TILES)
 QKV_TILES = (QKV // TILE_ROWS) * (D // LANES)
 OUT_TILES = (HEADS * HD // TILE_ROWS) * (D // LANES)
-MOE_CHAINS = (224, 224, 224, 192)
-ATTN_CHAINS = (64, 32, 32, 32)
-CHAINS = MOE_CHAINS + ATTN_CHAINS
-TILES = sum(CHAINS)
-ORDERS = (
-    ("core", "xa", "xb", "ya", "yb", "za", "zb"),
-    ("core", "xb", "xa", "yb", "ya", "zb", "za"),
-    ("core", "ya", "yb", "xa", "xb", "za", "zb"),
-    ("core", "yb", "ya", "xb", "xa", "zb", "za"),
-)
-HALVINGS = 5
-STEPS = 7
-LANDING = sum(c // 2 + c // 4 + c // 8 + c // 16 + 3 * (c // 32) for c in CHAINS)
-SMALL_ORDER = ("pair", "core", "xa", "xb", "ya", "yb", "za", "zb")
-SMALL_ROWS = 24
-SHARED_ROWS = 16
+BATCHES = ((128, 160),) * EXPERTS + ((64, 96),)
+CHAIN_COUNT = 2 * len(BATCHES)
+TILES = sum(sum(batch) for batch in BATCHES)
+ORDERS = (("core", "x", "y", "z"), ("core", "y", "x", "z"))
+GROUP = {"pair": 2, "core": 2, "x": RING, "y": RING, "z": RING}
+PHASES = 4
+LANDING = sum(c // 2 + 3 * (c // 8) + 7 * (c // 32) for batch in BATCHES for c in batch)
+SMALL_ORDER = ("pair", "core", "x", "y", "z")
+EARLY_ROWS, LATE_ROWS = 24, 16
+SHARED_ROWS = (16, 8)
 F32 = jnp.float32
 BF16 = jnp.bfloat16
 HIGHEST = lax.Precision.HIGHEST
 
 
-def partners():
+def places():
     me = lax.axis_index("dp")
-    core = me % 2
-    x = (me // 2) % RING
-    z = (me // (2 * RING)) % RING
-    y = me // (2 * RING * RING)
-
-    def dp_index(y, z, x, core):
-        return ((y * RING + z) * RING + x) * 2 + core
-
-    def swap(v):
-        return v + 1 - 2 * (v % 2)
-
-    return {
-        "core": ({"dp": dp_index(y, z, x, 1 - core)}, core),
-        "xa": ({"dp": dp_index(y, z, swap(x), core)}, (x + 1) // 2 % 2),
-        "xb": ({"dp": dp_index(y, z, RING - 1 - x, core)}, x // 2),
-        "ya": ({"dp": dp_index(swap(y), z, x, core)}, (y + 1) // 2 % 2),
-        "yb": ({"dp": dp_index(RING - 1 - y, z, x, core)}, y // 2),
-        "za": ({"dp": dp_index(y, swap(z), x, core)}, (z + 1) // 2 % 2),
-        "zb": ({"dp": dp_index(y, RING - 1 - z, x, core)}, z // 2),
-        "pair": ({"tensor": 1 - lax.axis_index("tensor")}, lax.axis_index("tensor")),
+    tensor = lax.axis_index("tensor")
+    at = {
+        "pair": tensor,
+        "core": me % 2,
+        "x": (me // 2) % RING,
+        "z": (me // (2 * RING)) % RING,
+        "y": me // (2 * RING * RING),
     }
+
+    def ahead(axis, distance):
+        if axis == "pair":
+            return {"tensor": 1 - tensor}
+        to = dict(at)
+        to[axis] = (at[axis] + distance) % GROUP[axis]
+        return {"dp": ((to["y"] * RING + to["z"]) * RING + to["x"]) * 2 + to["core"]}
+
+    return at, ahead
 
 
 def dot(a, b, dims=((1,), (0,)), precision=None):
@@ -95,14 +85,16 @@
     return jnp.sum(v, axis=0, keepdims=True)
 
 
-def add_tiles(ref, at, landing, landing_at, count):
+def add_tiles(out, at, count, parts):
     step = max(k for k in range(1, 17) if count % k == 0)
 
     @pl.loop(0, count // step)
     def _(i):
-        rows = pl.ds(at + i * step, step)
-        total = ref[rows].astype(F32) + landing[pl.ds(landing_at + i * step, step)].astype(F32)
-        ref[rows] = total.astype(ref.dtype)
+        total = None
+        for ref, start in parts:
+            piece = ref[pl.ds(start + i * step, step)].astype(F32)
+            total = piece if total is None else total + piece
+        out[pl.ds(at + i * step, step)] = total.astype(out.dtype)
 
 
 def store_tiles(ref, at, value):
@@ -121,27 +113,34 @@
     tok_ref,
     attn_gain_ref,
     attn_shift_ref,
-    w_qkv_ref,
+    w_qkv_hbm,
     qv_bias_ref,
-    w_out_ref,
+    w_out_hbm,
     out_bias_ref,
     moe_gain_ref,
     moe_shift_ref,
     router_ref,
-    w_in_ref,
+    w_in_hbm,
     in_bias_ref,
-    w_exp_ref,
+    w_exp_hbm,
     exp_bias_ref,
     route_ref,
     cot_ref,
     block_ref,
     grad_tok_ref,
-    sum_ref,
+    sum_out,
     small_out,
+    w_qkv_ref,
+    w_out_ref,
+    w_in_ref,
+    w_exp_ref,
     held,
     landing,
-    small_held,
-    small_landing,
+    sum_ref,
+    early_held,
+    early_landing,
+    late_held,
+    late_landing,
     normed,
     cots,
     moes,
@@ -177,19 +176,31 @@
     back_recv,
     small_send,
     small_recv,
+    load_sem,
+    store_sem,
 ):
-    who = partners()
+    place, ahead = places()
     barrier = pltpu.get_barrier_semaphore()
-    for device, _ in who.values():
-        pl.semaphore_signal(barrier, inc=1, device_id=device, device_id_type=MESH)
-
-    def remote(src, dst, send, recv, name):
+    peers = [(axis, d) for axis, group in GROUP.items() for d in range(1, group)]
+    for axis, d in peers:
+        pl.semaphore_signal(barrier, inc=1, device_id=ahead(axis, d), device_id_type=MESH)
+    loads = []
+    for src, dst in (
+        (w_qkv_hbm, w_qkv_ref),
+        (w_out_hbm, w_out_ref),
+        (w_in_hbm, w_in_ref),
+        (w_exp_hbm, w_exp_ref),
+    ):
+        loads.append(pltpu.make_async_copy(src, dst, load_sem.at[len(loads)]))
+        loads[-1].start()
+
+    def remote(src, dst, send, recv, axis, distance=1):
         copy = pltpu.make_async_remote_copy(
             src_ref=src,
             dst_ref=dst,
             send_sem=send,
             recv_sem=recv,
-            device_id=who[name][0],
+            device_id=ahead(axis, distance),
             device_id_type=MESH,
         )
         copy.start()
@@ -203,79 +214,161 @@
         return copy
 
     spots = [0]
+    stores = []
 
     class Chain:
-        def __init__(self, c):
-            self.c, self.order = c, ORDERS[c % len(ORDERS)]
-            self.base, self.size, self.k = sum(CHAINS[:c]), CHAINS[c], 0
+        def __init__(self, c, base, size):
+            self.c, self.base, self.size, self.order = c, base, size, ORDERS[c % 2]
+            self.first, self.whole = base, size
+            self.k, self.back, self.copies = 0, PHASES - 1, []
 
         def send(self):
-            c, k = self.c, self.k
-            name = self.order[k]
-            give = self.base
-            if k < HALVINGS:
-                self.size //= 2
-                bit = who[name][1]
-                give = self.base + (1 - bit) * self.size
-                self.base = self.base + bit * self.size
-            self.spot = spots[0]
-            spots[0] += self.size
-            self.copy = remote(
-                held.at[pl.ds(give, self.size)],
-                landing.at[pl.ds(self.spot, self.size)],
-                send_sem.at[c, k],
-                recv_sem.at[c, k],
-                name,
-            )
-
-        def send_back(self, k):
-            self.back = k
+            axis = self.order[self.k]
+            group, index = GROUP[axis], place[axis]
+            self.spot, earlier, self.copies = spots[0], self.copies, []
+            if axis == "z":
+                n = self.size
+                add_tiles(landing, self.spot + index * n, n, [(held, self.base)])
+                spots[0] += group * n
+            else:
+                n = self.size // group
+                spots[0] += (group - 1) * n
+            for d in range(1, group):
+                if axis == "z":
+                    src, dst = self.base, self.spot + index * n
+                else:
+                    src, dst = self.base + (index + d) % group * n, self.spot + (d - 1) * n
+                self.copies.append(
+                    remote(
+                        held.at[pl.ds(src, n)],
+                        landing.at[pl.ds(dst, n)],
+                        send_sem.at[self.c, self.k, d - 1],
+                        recv_sem.at[self.c, self.k, d - 1],
+                        axis,
+                        d,
+                    )
+                )
+            if axis != "z":
+                self.base, self.size = self.base + index * n, n
+            for copy in earlier:
+                copy.wait_send()
+
+        def send_back(self):
+            axis = self.order[self.back]
+            earlier, self.copies = self.copies, []
             part = sum_ref.at[pl.ds(self.base, self.size)]
-            self.copy = remote(
-                part, part, back_send.at[self.c, k], back_recv.at[self.c, k], self.order[k]
-            )
-            unsent.append(self.copy)
+            for d in range(1, GROUP[axis]):
+                self.copies.append(
+                    remote(
+                        part,
+                        part,
+                        back_send.at[self.c, self.back, d - 1],
+                        back_recv.at[self.c, self.back, d - 1],
+                        axis,
+                        d,
+                    )
+                )
+            for copy in earlier:
+                copy.wait_send()
 
         def advance(self):
-            if self.k < STEPS:
-                self.copy.wait_recv()
-                if self.k < HALVINGS:
-                    unsent.append(self.copy)
+            for copy in self.copies:
+                copy.wait_recv()
+            if self.k < PHASES:
+                axis = self.order[self.k]
+                n = self.size
+                if axis == "z":
+                    parts = [(landing, self.spot + j * n) for j in range(GROUP[axis])]
+                    add_tiles(sum_ref, self.base, n, parts)
                 else:
-                    self.copy.wait_send()
-                add_tiles(held, self.base, landing, self.spot, self.size)
+                    parts = [(landing, self.spot + j * n) for j in range(GROUP[axis] - 1)]
+                    add_tiles(held, self.base, n, [(held, self.base)] + parts)
                 self.k += 1
-                if self.k < STEPS:
+                if self.k < PHASES:
                     self.send()
                     return
-                step = max(k for k in range(1, 17) if self.size % k == 0)
-
-                @pl.loop(0, self.size // step)
-                def _(i):
-                    rows = pl.ds(self.base + i * step, step)
-                    sum_ref[rows] = held[rows]
-
-                self.send_back(HALVINGS - 1)
-            elif self.back >= 0:
-                self.copy.wait_recv()
-                self.base = self.base - who[self.order[self.back]][1] * self.size
-                self.size = self.size * 2
-                if self.back:
-                    self.send_back(self.back - 1)
-                else:
-                    self.back = -1
-
-    def small_step(k):
-        rows = SHARED_ROWS if k == 0 else SMALL_ROWS
-        copy = remote(
-            small_held.at[k, pl.ds(0, rows)],
-            small_landing.at[k, pl.ds(0, rows)],
-            small_send.at[k],
-            small_recv.at[k],
-            SMALL_ORDER[k],
-        )
-        unsent.append(copy)
-        return copy
+            else:
+                axis = self.order[self.back]
+                self.base = self.base - place[axis] * self.size
+                self.size = self.size * GROUP[axis]
+            self.back -= 1
+            if self.back >= 0:
+                self.send_back()
+                return
+            rows = pl.ds(self.first, self.whole)
+            copy = pltpu.make_async_copy(
+                sum_ref.at[rows], sum_out.at[rows], store_sem.at[self.c]
+            )
+            copy.start()
+            stores.append(copy)
+            for copy in self.copies:
+                copy.wait_send()
+
+    class Small:
+        def __init__(self, b, held, landing, rows):
+            self.b, self.held, self.landing, self.rows = b, held, landing, rows
+            self.k, self.copies = 0, []
+
+        def send(self):
+            k, axis = self.k, SMALL_ORDER[self.k]
+            group, index = GROUP[axis], place[axis]
+            n = SHARED_ROWS[self.b] if axis == "pair" else self.rows
+            earlier, self.copies = self.copies, []
+            slot = 0
+            if group > 2:
+                slot = index
+                self.landing[k, slot] = self.held[k]
+            for d in range(1, group):
+                self.copies.append(
+                    remote(
+                        self.held.at[k, pl.ds(0, n)],
+                        self.landing.at[k, slot, pl.ds(0, n)],
+                        small_send.at[self.b, k, d - 1],
+                        small_recv.at[self.b, k, d - 1],
+                        axis,
+                        d,
+                    )
+                )
+            for copy in earlier:
+                copy.wait_send()
+
+        def advance(self):
+            for copy in self.copies:
+                copy.wait_recv()
+            k, axis = self.k, SMALL_ORDER[self.k]
+            held, landing = self.held, self.landing
+            if axis == "pair":
+                n = SHARED_ROWS[self.b]
+                held[k + 1, :n] = held[k, :n] + landing[k, 0, :n]
+                held[k + 1, n:] = held[k, n:]
+            elif GROUP[axis] == 2:
+                held[k + 1] = held[k] + landing[k, 0]
+            else:
+                held[k + 1] = landing[k, 0] + landing[k, 1] + landing[k, 2] + landing[k, 3]
+            self.k += 1
+            if self.k < len(SMALL_ORDER):
+                self.send()
+                return
+            small_out[EARLY_ROWS * self.b : EARLY_ROWS * self.b + self.rows] = held[self.k]
+            for copy in self.copies:
+                copy.wait_send()
+
+    early = Small(0, early_held, early_landing, EARLY_ROWS)
+    late = Small(1, late_held, late_landing, LATE_ROWS)
+    batches, start = [], 0
+    for batch in BATCHES:
+        batches.append([])
+        for size in batch:
+            batches[-1].append(Chain(2 * len(batches) - 2 + len(batches[-1]), start, size))
+            start += size
+
+    def send_batch(b):
+        for chain in batches[b]:
+            chain.send()
+
+    def advance_batch(b):
+        for chain in batches[b]:
+            chain.advance()
 
     def row_of(ref):
         return ref[...].astype(F32).reshape(1, D)
@@ -292,7 +385,7 @@
     attn_xhat[...] = xhat
     normed[0] = (xhat * attn_gain + attn_shift).astype(BF16)
     cots[0] = padded[1].astype(BF16)
-    pl.semaphore_wait(barrier, len(who))
+    pl.semaphore_wait(barrier, len(peers))
     normed_copy = exchange(0, normed.at[0], normed.at[1])
     cot_copy = exchange(1, cots.at[0], cots.at[1])
 
@@ -358,6 +451,8 @@
     def dispatch_t(i, e):
         return (pos_row[i][e : e + 1] == slot_sub).astype(F32)
 
+    loads[0].wait()
+    loads[1].wait()
     project(0)
     normed_copy.wait_recv()
     project(1)
@@ -403,7 +498,9 @@
     fill_slots(1)
 
     gate_rows = [[None] * EXPERTS, [None] * EXPERTS]
-    small_held[0] = jnp.zeros((SMALL_ROWS, D), F32)
+    early_held[0] = jnp.zeros((EARLY_ROWS, D), F32)
+    loads[2].wait()
+    loads[3].wait()
     for e in range(EXPERTS):
         weight = jnp.concatenate([slot_weight[0][e], slot_weight[1][e]], axis=0)
         pre = dot(slot_in[e], w_in_ref[e]) + in_bias_ref[e : e + 1].astype(F32)
@@ -424,6 +521,14 @@
                 dispatch_t(i, e) * slot_gate[i * CAP : (i + 1) * CAP]
             )
 
+        at = e * (IN_TILES + EXP_TILES)
+        store_tiles(held, at, dot(slot_in[e], gpre_all[e], FIRST))
+        store_tiles(held, at + IN_TILES, dot(act_all[e], gslot_all[e], FIRST))
+        bias = column_sum(gpre_all[e].astype(F32))
+        for j in range(FF // D):
+            early_held[0, 16 + 2 * e + j : 17 + 2 * e + j] = bias[:, j * D : (j + 1) * D]
+        send_batch(e)
+
     def combine(i, ref):
         total = jnp.zeros((ROWS, D), F32)
         for e in range(EXPERTS):
@@ -441,17 +546,7 @@
     mix_copy = exchange(6, mix_part.at[0], mix_part.at[1])
 
     for e in range(EXPERTS):
-        at = e * (IN_TILES + EXP_TILES)
-        store_tiles(held, at, dot(slot_in[e], gpre_all[e], FIRST))
-        store_tiles(held, at + IN_TILES, dot(act_all[e], gslot_all[e], FIRST))
-        bias = column_sum(gpre_all[e].astype(F32))
-        for j in range(FF // D):
-            small_held[0, 16 + 2 * e + j : 17 + 2 * e + j] = bias[:, j * D : (j + 1) * D]
-    chains = [Chain(c) for c in range(len(CHAINS))]
-    moe_chains = chains[: len(MOE_CHAINS)]
-    attn_chains = chains[len(MOE_CHAINS) :]
-    for chain in moe_chains:
-        chain.send()
+        advance_batch(e)
 
     own_gmoe = combine(0, gback_all).astype(BF16).astype(F32)
     own_mix = combine(0, scaled_all).astype(BF16).astype(F32)
@@ -465,25 +560,24 @@
     gate_copy.wait_recv()
     grad_gates = (own_gate + gate_part[1] + bias_grad) * kept_row[0]
     grad_logits = gates[0] * (grad_gates - column_sum(gates[0] * grad_gates))
-    small_held[0, 5:8] = dot(grad_logits, moes[0].astype(F32), precision=HIGHEST)[:EXPERTS]
-    small_held[0, 8:11] = dot(share, cot, precision=HIGHEST)[:EXPERTS]
+    early_held[0, 3:6] = dot(grad_logits, moes[0].astype(F32), precision=HIGHEST)[:EXPERTS]
+    early_held[0, 6:9] = dot(share, cot, precision=HIGHEST)[:EXPERTS]
     router_back = dot(grad_logits, router_rows, FIRST, HIGHEST)
     gmoe_copy.wait_recv()
     gmoe = own_gmoe + gmoe_part[1].astype(F32) + router_back
     grad_hidden = cot + norm_back(gmoe, moe_xhat[...], moe_r, moe_gain)
     ghs[0] = grad_hidden.astype(BF16)
     gh_copy = exchange(7, ghs.at[0], ghs.at[1])
-    small_held[0, 2:3] = column_sum(grad_hidden)
-    small_held[0, 3:4] = column_sum(gmoe * moe_xhat[...])
-    small_held[0, 4:5] = column_sum(gmoe)
+    early_held[0, 0:1] = column_sum(grad_hidden)
+    early_held[0, 1:2] = column_sum(gmoe * moe_xhat[...])
+    early_held[0, 2:3] = column_sum(gmoe)
+    early.send()
     mix_copy.wait_recv()
     block_ref[...] = (
         hidden_ref[...]
         + (own_mix + mix_part[1].astype(F32))
         + dot(share, bias_rows.astype(F32), FIRST, HIGHEST)
     ).astype(BF16)
-    for chain in moe_chains:
-        chain.advance()
 
     def attend_back(i):
         for h in range(HEADS):
@@ -516,41 +610,35 @@
             held[spot : spot + HD // TILE_ROWS] = tiles.reshape(HD // TILE_ROWS, TILE_ROWS, LANES)
     at += OUT_TILES
     held[at:TILES] = jnp.zeros((TILES - at, TILE_ROWS, LANES), BF16)
-    for chain in attn_chains:
-        chain.send()
+    send_batch(EXPERTS)
+    late_held[0] = jnp.zeros((LATE_ROWS, D), F32)
     bias = column_sum(both.astype(F32))
-    small_held[0, 22:23] = bias[:, :D]
-    small_held[0, 23:24, 0 : QKV - D] = bias[:, D:]
-    for chain in moe_chains:
-        chain.advance()
+    late_held[0, 8:9] = bias[:, :D]
+    late_held[0, 9:10, 0 : QKV - D] = bias[:, D:]
+    for e in range(EXPERTS):
+        advance_batch(e)
+    early.advance()
 
     own_gnorm = dot(gproj[0], w_qkv_ref[...]).astype(BF16).astype(F32)
     gnorm_copy.wait_recv()
     gnorm = own_gnorm + gnorm_part[1].astype(F32)
     xhat = attn_xhat[...]
-    small_held[0, 0:1] = column_sum(gnorm * xhat)
-    small_held[0, 1:2] = column_sum(gnorm)
-    small_copy = small_step(0)
+    late_held[0, 0:1] = column_sum(gnorm * xhat)
+    late_held[0, 1:2] = column_sum(gnorm)
+    late.send()
     grad_tok_ref[...] = (grad_hidden + norm_back(gnorm, xhat, attn_r, attn_gain)).astype(BF16)
 
-    for k in range(STEPS + HALVINGS):
-        for chain in attn_chains:
-            chain.advance()
-        for chain in moe_chains:
-            chain.advance()
+    for k in range(2 * PHASES - 1):
+        if k < 2 * PHASES - 3:
+            for e in range(EXPERTS):
+                advance_batch(e)
+        advance_batch(EXPERTS)
+        if k < len(SMALL_ORDER) - 1:
+            early.advance()
         if k < len(SMALL_ORDER):
-            small_copy.wait_recv()
-            if k == 0:
-                small_held[1, :SHARED_ROWS] = (
-                    small_held[0, :SHARED_ROWS] + small_landing[0, :SHARED_ROWS]
-                )
-                small_held[1, SHARED_ROWS:] = small_held[0, SHARED_ROWS:]
-            elif k < len(SMALL_ORDER) - 1:
-                small_held[k + 1] = small_held[k] + small_landing[k]
-            else:
-                small_out[...] = small_held[k] + small_landing[k]
-            if k < len(SMALL_ORDER) - 1:
-                small_copy = small_step(k + 1)
+            late.advance()
+    for copy in stores:
+        copy.wait()
     for copy in unsent:
         copy.wait_send()
 
@@ -563,23 +651,32 @@
         return pltpu.VMEM(shape, F32)
 
     dma = pltpu.SemaphoreType.DMA
-    count = len(CHAINS)
     slots = 2 * CAP
+    steps = len(SMALL_ORDER)
+    vmem = pl.BlockSpec(memory_space=pltpu.VMEM)
+    anywhere = pl.BlockSpec(memory_space=pl.ANY)
     return pl.pallas_call(
         block_kernel,
         out_shape=(
             jax.ShapeDtypeStruct((ROWS, D), BF16),
             jax.ShapeDtypeStruct((ROWS, D), BF16),
             jax.ShapeDtypeStruct((TILES, TILE_ROWS, LANES), BF16),
-            jax.ShapeDtypeStruct((SMALL_ROWS, D), F32),
+            jax.ShapeDtypeStruct((EARLY_ROWS + LATE_ROWS, D), F32),
         ),
-        in_specs=[pl.BlockSpec(memory_space=pltpu.VMEM)] * len(args),
-        out_specs=[pl.BlockSpec(memory_space=pltpu.VMEM)] * 4,
+        in_specs=[anywhere if i in (3, 5, 10, 12) else vmem for i in range(len(args))],
+        out_specs=[vmem, vmem, anywhere, vmem],
         scratch_shapes=[
+            bf(QKV, D),
+            bf(HEADS * HD, D),
+            bf(EXPERTS, D, FF),
+            bf(EXPERTS, FF, D),
             bf(TILES, TILE_ROWS, LANES),
             bf(LANDING, TILE_ROWS, LANES),
-            fl(STEPS + 1, SMALL_ROWS, D),
-            fl(STEPS + 1, SMALL_ROWS, D),
+            bf(TILES, TILE_ROWS, LANES),
+            fl(steps + 1, EARLY_ROWS, D),
+            fl(steps, RING, EARLY_ROWS, D),
+            fl(steps + 1, LATE_ROWS, D),
+            fl(steps, RING, LATE_ROWS, D),
             bf(2, ROWS, D),
             bf(2, ROWS, D),
             bf(2, ROWS, D),
@@ -609,12 +706,14 @@
             fl(2, 2, ROWS),
             dma((9,)),
             dma((9,)),
-            dma((count, STEPS)),
-            dma((count, STEPS)),
-            dma((count, HALVINGS)),
-            dma((count, HALVINGS)),
-            dma((STEPS + 1,)),
-            dma((STEPS + 1,)),
+            dma((CHAIN_COUNT, PHASES, RING - 1)),
+            dma((CHAIN_COUNT, PHASES, RING - 1)),
+            dma((CHAIN_COUNT, PHASES - 1, RING - 1)),
+            dma((CHAIN_COUNT, PHASES - 1, RING - 1)),
+            dma((2, steps, RING - 1)),
+            dma((2, steps, RING - 1)),
+            dma((4,)),
+            dma((CHAIN_COUNT,)),
         ],
         compiler_params=pltpu.CompilerParams(
             collective_id=0, has_side_effects=True, vmem_limit_bytes=56 * 1024 * 1024
@@ -666,14 +765,15 @@
     block_out[0] = block_ref[:SEQ]
     grad_tok_out[0] = grad_tok_ref[:SEQ]
     small = small_ref[...]
-    for ref, row in zip((attn_gain, attn_shift, out_bias, moe_gain, moe_shift), range(5)):
+    rows = (24, 25, 0, 1, 2)
+    for ref, row in zip((attn_gain, attn_shift, out_bias, moe_gain, moe_shift), rows):
         ref[...] = small[row]
-    router[...] = small[5:8]
-    exp_bias[...] = small[8:11]
+    router[...] = small[3:6]
+    exp_bias[...] = small[6:9]
     for e in range(EXPERTS):
         for j in range(FF // D):
             in_bias[e : e + 1, j * D : (j + 1) * D] = small[16 + 2 * e + j : 17 + 2 * e + j]
-    bias = jnp.concatenate([small[22:23], small[23:24]], axis=1)
+    bias = jnp.concatenate([small[32:33], small[33:34]], axis=1)
     for h in range(HEADS):
         at = 3 * h * HD
         qv_bias[h : h + 1, :HD] = bias[:, at : at + HD]
@@ -730,7 +830,7 @@
             pltpu.SemaphoreType.DMA((8,)),
             pltpu.SemaphoreType.DMA((8,)),
         ],
-        compiler_params=pltpu.CompilerParams(vmem_limit_bytes=40 * 1024 * 1024),
+        compiler_params=pltpu.CompilerParams(vmem_limit_bytes=58 * 1024 * 1024),
     )(*args)
 
 

time: 104 us -> 95.4 us (0.917)
  local copies, waits for them, and re-layouts: 4.78 us -> 0 us
  Pallas kernels: 98.1 us -> 94.4 us
    unnamed x8 -> x0, local copies, waits for them, and re-layouts: 4.78 us -> none
    pallas_call x1, Pallas kernels: 92.5 us -> 88.2 us  [run_block(): pl.pallas_call(block_kernel, out_shape=(jax.ShapeDtypeStruct((ROWS, D), B...]
where the time goes in v3:
time: 95.4 us; the launch traced here: 95.2 us
  Pallas kernels  94.4 us (99%)
    pallas_call x1, Pallas kernels, run_block(): pl.pallas_call(block_kernel, out_shape=(jax.ShapeDtypeStruct((ROWS, D), B...  88.2 us
    pallas_call x1, Pallas kernels, unpack(): pl.pallas_call(unpack_kernel, out_shape=shapes, in_specs=[vmem, vmem, any...  6.27 us

profile of v3, /device:TPU:1, one launch (start us, length us, event | category | flops | bytes accessed | tf_op | source)
XLA Modules:
  0.0 95.2 jit_solution(6381787982602476006)
XLA Ops:
  0.7 88.2 %shard_map.271 = (bf16[208,384]{1,0:T(8,128)(2,1)}, bf16[208,384]{1,0:T(8,128)(2,1)}, bf16[1024,16,128]{2,1,0:T(8,128)(2,1)}, f32[40,384]{1,0:T(8,128)}) custom-call(bf16[1,197,384]{2,1,0:T(8,128)(2,1)} %tok_ref.1, f32[384]{0:T(512)} %attn_gain_ref.1, f32[384]{0:T(512)} %attn_shift_ref.1, bf16[576,384]{1,0:T(8,128)(2,1)} %bitcast.11, ...), custom_call_target="tpu_custom_call" | custom-call | tf_op jit(solution)/shard_map/pallas_call | solution.py:658
  88.8 6.3 %shard_map.272 = (bf16[1,197,384]{2,1,0:T(8,128)(2,1)}, bf16[1,197,384]{2,1,0:T(8,128)(2,1)}, f32[384]{0:T(512)}, f32[384]{0:T(512)}, f32[576,384]{1,0:T(8,128)}...) custom-call(bf16[208,384]{1,0:T(8,128)(2,1)} %get-tuple-element.34.b, ...), custom_call_target="tpu_custom_call" | custom-call | tf_op jit(solution)/shard_map/pallas_call | solution.py:819

commit v4 on v3

--- a/solution.py
+++ b/solution.py
@@ -28,8 +28,8 @@
 PHASES = 4
 LANDING = sum(c // 2 + 3 * (c // 8) + 7 * (c // 32) for batch in BATCHES for c in batch)
 SMALL_ORDER = ("pair", "core", "x", "y", "z")
-EARLY_ROWS, LATE_ROWS = 24, 16
-SHARED_ROWS = (16, 8)
+EARLY_ROWS, LATE_ROWS = 16, 8
+SHARED_ROWS = (9, 2)
 F32 = jnp.float32
 BF16 = jnp.bfloat16
 HIGHEST = lax.Precision.HIGHEST
@@ -109,20 +109,49 @@
         ref[at + j * per : at + (j + 1) * per] = part.astype(BF16).reshape(per, TILE_ROWS, LANES)
 
 
-def block_kernel(
+def block_kernel(*refs):
+    count = 16
+    sources, (block_out, grad_tok_out, sum_out, small_hbm) = refs[:count], refs[count : count + 4]
+    inputs = refs[count + 4 : 2 * count + 4]
+    results = refs[2 * count + 4 : 2 * count + 7]
+    work = refs[2 * count + 7 : -2]
+    load_sem, result_sem = refs[-2:]
+    loads = [
+        pltpu.make_async_copy(src, dst, load_sem.at[i])
+        for i, (src, dst) in enumerate(zip(sources, inputs))
+    ]
+    stores = []
+
+    def store(i, out):
+        copy = pltpu.make_async_copy(results[i], out, result_sem.at[i])
+        copy.start()
+        stores.append(copy)
+
+    finish = (
+        lambda: store(0, block_out),
+        lambda: store(1, grad_tok_out),
+        lambda: store(2, small_hbm),
+    )
+    block_body(loads, stores, finish, *inputs, *results[:2], sum_out, results[2], *work)
+
+
+def block_body(
+    loads,
+    stores,
+    finish,
     tok_ref,
     attn_gain_ref,
     attn_shift_ref,
-    w_qkv_hbm,
+    w_qkv_ref,
     qv_bias_ref,
-    w_out_hbm,
+    w_out_ref,
     out_bias_ref,
     moe_gain_ref,
     moe_shift_ref,
     router_ref,
-    w_in_hbm,
+    w_in_ref,
     in_bias_ref,
-    w_exp_hbm,
+    w_exp_ref,
     exp_bias_ref,
     route_ref,
     cot_ref,
@@ -130,10 +159,6 @@
     grad_tok_ref,
     sum_out,
     small_out,
-    w_qkv_ref,
-    w_out_ref,
-    w_in_ref,
-    w_exp_ref,
     held,
     landing,
     sum_ref,
@@ -141,14 +166,18 @@
     early_landing,
     late_held,
     late_landing,
+    toks,
     normed,
     cots,
     moes,
     ghs,
     att_part,
+    att_other,
     mix_part,
     gmoe_part,
+    gmoe_other,
     gate_part,
+    gate_other,
     gnorm_part,
     q_all,
     k_all,
@@ -166,6 +195,7 @@
     attn_xhat,
     moe_xhat,
     hidden_ref,
+    gh_ref,
     padded,
     route_pad,
     pair_send,
@@ -176,7 +206,6 @@
     back_recv,
     small_send,
     small_recv,
-    load_sem,
     store_sem,
 ):
     place, ahead = places()
@@ -184,15 +213,9 @@
     peers = [(axis, d) for axis, group in GROUP.items() for d in range(1, group)]
     for axis, d in peers:
         pl.semaphore_signal(barrier, inc=1, device_id=ahead(axis, d), device_id_type=MESH)
-    loads = []
-    for src, dst in (
-        (w_qkv_hbm, w_qkv_ref),
-        (w_out_hbm, w_out_ref),
-        (w_in_hbm, w_in_ref),
-        (w_exp_hbm, w_exp_ref),
-    ):
-        loads.append(pltpu.make_async_copy(src, dst, load_sem.at[len(loads)]))
-        loads[-1].start()
+    big = (3, 5, 10, 12)
+    for i in [i for i in range(len(loads)) if i not in big] + list(big):
+        loads[i].start()
 
     def remote(src, dst, send, recv, axis, distance=1):
         copy = pltpu.make_async_remote_copy(
@@ -214,7 +237,6 @@
         return copy
 
     spots = [0]
-    stores = []
 
     class Chain:
         def __init__(self, c, base, size):
@@ -312,7 +334,6 @@
         def send(self):
             k, axis = self.k, SMALL_ORDER[self.k]
             group, index = GROUP[axis], place[axis]
-            n = SHARED_ROWS[self.b] if axis == "pair" else self.rows
             earlier, self.copies = self.copies, []
             slot = 0
             if group > 2:
@@ -321,8 +342,8 @@
             for d in range(1, group):
                 self.copies.append(
                     remote(
-                        self.held.at[k, pl.ds(0, n)],
-                        self.landing.at[k, slot, pl.ds(0, n)],
+                        self.held.at[k],
+                        self.landing.at[k, slot],
                         small_send.at[self.b, k, d - 1],
                         small_recv.at[self.b, k, d - 1],
                         axis,
@@ -338,9 +359,9 @@
             k, axis = self.k, SMALL_ORDER[self.k]
             held, landing = self.held, self.landing
             if axis == "pair":
-                n = SHARED_ROWS[self.b]
-                held[k + 1, :n] = held[k, :n] + landing[k, 0, :n]
-                held[k + 1, n:] = held[k, n:]
+                row = lax.broadcasted_iota(jnp.int32, (self.rows, D), 0)
+                other = jnp.where(row < SHARED_ROWS[self.b], landing[k, 0], 0.0)
+                held[k + 1] = held[k] + other
             elif GROUP[axis] == 2:
                 held[k + 1] = held[k] + landing[k, 0]
             else:
@@ -370,6 +391,10 @@
         for chain in batches[b]:
             chain.advance()
 
+    for i in range(len(loads)):
+        if i not in big:
+            loads[i].wait()
+
     def row_of(ref):
         return ref[...].astype(F32).reshape(1, D)
 
@@ -380,14 +405,14 @@
     padded[:, SEQ - 5 :] = jnp.zeros((2, ROWS - SEQ + 5, D), F32)
     padded[0, :SEQ] = tok_ref[0].astype(F32)
     padded[1, :SEQ] = cot_ref[0].astype(F32)
-    tok = padded[0]
-    xhat, attn_r = normalize(tok)
+    toks[0] = padded[0].astype(BF16)
+    cots[0] = padded[1].astype(BF16)
+    pl.semaphore_wait(barrier, len(peers))
+    tok_copy = exchange(0, toks.at[0], toks.at[1])
+    cot_copy = exchange(1, cots.at[0], cots.at[1])
+    xhat, attn_r = normalize(padded[0])
     attn_xhat[...] = xhat
     normed[0] = (xhat * attn_gain + attn_shift).astype(BF16)
-    cots[0] = padded[1].astype(BF16)
-    pl.semaphore_wait(barrier, len(peers))
-    normed_copy = exchange(0, normed.at[0], normed.at[1])
-    cot_copy = exchange(1, cots.at[0], cots.at[1])
 
     key_mask = lax.broadcasted_iota(jnp.int32, (ROWS, ROWS), 1) < SEQ
 
@@ -451,27 +476,32 @@
     def dispatch_t(i, e):
         return (pos_row[i][e : e + 1] == slot_sub).astype(F32)
 
-    loads[0].wait()
-    loads[1].wait()
+    loads[3].wait()
+    loads[5].wait()
     project(0)
-    normed_copy.wait_recv()
+    att_part[0] = attend(0).astype(BF16)
+    att_copies = [exchange(2, att_part.at[0], att_other.at[1])]
+    tok_copy.wait_recv()
+    normed[1] = (normalize(toks[1].astype(F32))[0] * attn_gain + attn_shift).astype(BF16)
     project(1)
-    att_part[0] = attend(1).astype(BF16)
-    att_copy = exchange(2, att_part.at[0], att_part.at[1])
-    own_part = attend(0)
+    att_part[1] = attend(1).astype(BF16)
+    att_copies.append(exchange(3, att_part.at[1], att_other.at[0]))
     cot_copy.wait_recv()
     for i in range(2):
         for e in range(EXPERTS):
             slot_cot[e, i * CAP : (i + 1) * CAP] = dot(
                 dispatch_t(i, e).astype(BF16), cots[i]
             ).astype(BF16)
-    att_copy.wait_recv()
-    hidden = tok + (own_part.astype(BF16).astype(F32) + att_part[1].astype(F32)) + out_bias
-    hidden_ref[...] = hidden
-    xhat, moe_r = normalize(hidden)
-    moe_xhat[...] = xhat
-    moes[0] = (xhat * moe_gain + moe_shift).astype(BF16)
-    moe_copy = exchange(3, moes.at[0], moes.at[1])
+    moe_r = [None, None]
+
+    def norm_hidden(i):
+        total = att_part[i].astype(F32) + att_other[i].astype(F32)
+        hidden = toks[i].astype(F32) + total + out_bias
+        if i == 0:
+            hidden_ref[...] = hidden
+        xhat, moe_r[i] = normalize(hidden)
+        moe_xhat[i] = xhat
+        moes[i] = (xhat * moe_gain + moe_shift).astype(BF16)
 
     router_rows = jnp.concatenate(
         [router_ref[...].astype(F32), jnp.zeros((8 - EXPERTS, D), F32)], axis=0
@@ -493,14 +523,15 @@
             slot_in[e, i * CAP : (i + 1) * CAP] = dot(pick.astype(BF16), moes[i]).astype(BF16)
             slot_weight[i][e] = jnp.sum(pick * gates[i][e : e + 1], axis=1, keepdims=True)
 
-    fill_slots(0)
-    moe_copy.wait_recv()
-    fill_slots(1)
+    for i in (1, 0):
+        att_copies[1 - i].wait_recv()
+        norm_hidden(i)
+        fill_slots(i)
 
     gate_rows = [[None] * EXPERTS, [None] * EXPERTS]
     early_held[0] = jnp.zeros((EARLY_ROWS, D), F32)
-    loads[2].wait()
-    loads[3].wait()
+    loads[10].wait()
+    loads[12].wait()
     for e in range(EXPERTS):
         weight = jnp.concatenate([slot_weight[0][e], slot_weight[1][e]], axis=0)
         pre = dot(slot_in[e], w_in_ref[e]) + in_bias_ref[e : e + 1].astype(F32)
@@ -526,7 +557,7 @@
         store_tiles(held, at + IN_TILES, dot(act_all[e], gslot_all[e], FIRST))
         bias = column_sum(gpre_all[e].astype(F32))
         for j in range(FF // D):
-            early_held[0, 16 + 2 * e + j : 17 + 2 * e + j] = bias[:, j * D : (j + 1) * D]
+            early_held[0, 9 + 2 * e + j : 10 + 2 * e + j] = bias[:, j * D : (j + 1) * D]
         send_batch(e)
 
     def combine(i, ref):
@@ -538,46 +569,41 @@
     def gate_grads(i):
         return jnp.concatenate(gate_rows[i] + [jnp.zeros((8 - EXPERTS, ROWS), F32)], axis=0)
 
-    gmoe_part[0] = combine(1, gback_all).astype(BF16)
-    gmoe_copy = exchange(4, gmoe_part.at[0], gmoe_part.at[1])
-    gate_part[0] = gate_grads(1)
-    gate_copy = exchange(5, gate_part.at[0], gate_part.at[1])
+    gmoe_copies, gate_copies = [], []
+    for i in range(2):
+        gate_part[i] = gate_grads(i)
+        gate_copies.append(exchange(4 + i, gate_part.at[i], gate_other.at[1 - i]))
+        gmoe_part[i] = combine(i, gback_all).astype(BF16)
+        gmoe_copies.append(exchange(6 + i, gmoe_part.at[i], gmoe_other.at[1 - i]))
     mix_part[0] = combine(1, scaled_all).astype(BF16)
-    mix_copy = exchange(6, mix_part.at[0], mix_part.at[1])
-
+    mix_copy = exchange(8, mix_part.at[0], mix_part.at[1])
     for e in range(EXPERTS):
         advance_batch(e)
 
-    own_gmoe = combine(0, gback_all).astype(BF16).astype(F32)
     own_mix = combine(0, scaled_all).astype(BF16).astype(F32)
-    own_gate = gate_grads(0)
-    cot = padded[1]
     bias_rows = jnp.concatenate(
         [exp_bias_ref[...], jnp.zeros((8 - EXPERTS, D), BF16)], axis=0
     )
     share = gates[0] * kept_row[0]
-    bias_grad = dot(bias_rows, cots[0], LAST)
-    gate_copy.wait_recv()
-    grad_gates = (own_gate + gate_part[1] + bias_grad) * kept_row[0]
-    grad_logits = gates[0] * (grad_gates - column_sum(gates[0] * grad_gates))
-    early_held[0, 3:6] = dot(grad_logits, moes[0].astype(F32), precision=HIGHEST)[:EXPERTS]
-    early_held[0, 6:9] = dot(share, cot, precision=HIGHEST)[:EXPERTS]
-    router_back = dot(grad_logits, router_rows, FIRST, HIGHEST)
-    gmoe_copy.wait_recv()
-    gmoe = own_gmoe + gmoe_part[1].astype(F32) + router_back
-    grad_hidden = cot + norm_back(gmoe, moe_xhat[...], moe_r, moe_gain)
-    ghs[0] = grad_hidden.astype(BF16)
-    gh_copy = exchange(7, ghs.at[0], ghs.at[1])
-    early_held[0, 0:1] = column_sum(grad_hidden)
-    early_held[0, 1:2] = column_sum(gmoe * moe_xhat[...])
-    early_held[0, 2:3] = column_sum(gmoe)
-    early.send()
-    mix_copy.wait_recv()
-    block_ref[...] = (
-        hidden_ref[...]
-        + (own_mix + mix_part[1].astype(F32))
-        + dot(share, bias_rows.astype(F32), FIRST, HIGHEST)
-    ).astype(BF16)
+
+    def hidden_back(i):
+        bias_grad = dot(bias_rows, cots[i], LAST)
+        gate_copies[1 - i].wait_recv()
+        grad_gates = (gate_part[i] + gate_other[i] + bias_grad) * kept_row[i]
+        grad_logits = gates[i] * (grad_gates - column_sum(gates[i] * grad_gates))
+        router_back = dot(grad_logits, router_rows, FIRST, HIGHEST)
+        gmoe_copies[1 - i].wait_recv()
+        gmoe = gmoe_part[i].astype(F32) + gmoe_other[i].astype(F32) + router_back
+        grad = cots[i].astype(F32) + norm_back(gmoe, moe_xhat[i], moe_r[i], moe_gain)
+        ghs[i] = grad.astype(BF16)
+        if i == 0:
+            gh_ref[...] = grad
+            early_held[0, 0:1] = column_sum(grad)
+            early_held[0, 1:2] = column_sum(gmoe * moe_xhat[0])
+            early_held[0, 2:3] = column_sum(gmoe)
+            early_held[0, 3:6] = dot(grad_logits, moes[0].astype(F32), precision=HIGHEST)[:EXPERTS]
+            early_held[0, 6:9] = dot(share, padded[1], precision=HIGHEST)[:EXPERTS]
+            early.send()
 
     def attend_back(i):
         for h in range(HEADS):
@@ -591,11 +617,12 @@
             gproj[i, :, at + HD : at + 2 * HD] = dot(graw, q, FIRST).astype(BF16)
             gproj[i, :, at + 2 * HD : at + 3 * HD] = dot(p.astype(BF16), gc, FIRST).astype(BF16)
 
-    attend_back(0)
-    gh_copy.wait_recv()
+    hidden_back(1)
     attend_back(1)
     gnorm_part[0] = dot(gproj[1], w_qkv_ref[...]).astype(BF16)
-    gnorm_copy = exchange(8, gnorm_part.at[0], gnorm_part.at[1])
+    gnorm_copy = exchange(9, gnorm_part.at[0], gnorm_part.at[1])
+    hidden_back(0)
+    attend_back(0)
 
     both = gproj[...].reshape(2 * ROWS, QKV)
     at = MOE_TILES
@@ -613,11 +640,18 @@
     send_batch(EXPERTS)
     late_held[0] = jnp.zeros((LATE_ROWS, D), F32)
     bias = column_sum(both.astype(F32))
-    late_held[0, 8:9] = bias[:, :D]
-    late_held[0, 9:10, 0 : QKV - D] = bias[:, D:]
+    late_held[0, 2:3] = bias[:, :D]
+    late_held[0, 3:4, 0 : QKV - D] = bias[:, D:]
     for e in range(EXPERTS):
         advance_batch(e)
     early.advance()
+    mix_copy.wait_recv()
+    block_ref[...] = (
+        hidden_ref[...]
+        + (own_mix + mix_part[1].astype(F32))
+        + dot(share, bias_rows.astype(F32), FIRST, HIGHEST)
+    ).astype(BF16)
+    finish[0]()
 
     own_gnorm = dot(gproj[0], w_qkv_ref[...]).astype(BF16).astype(F32)
     gnorm_copy.wait_recv()
@@ -626,17 +660,19 @@
     late_held[0, 0:1] = column_sum(gnorm * xhat)
     late_held[0, 1:2] = column_sum(gnorm)
     late.send()
-    grad_tok_ref[...] = (grad_hidden + norm_back(gnorm, xhat, attn_r, attn_gain)).astype(BF16)
+    grad_tok_ref[...] = (gh_ref[...] + norm_back(gnorm, xhat, attn_r, attn_gain)).astype(BF16)
+    finish[1]()
 
     for k in range(2 * PHASES - 1):
+        advance_batch(EXPERTS)
         if k < 2 * PHASES - 3:
             for e in range(EXPERTS):
                 advance_batch(e)
-        advance_batch(EXPERTS)
+        if k < len(SMALL_ORDER):
+            late.advance()
         if k < len(SMALL_ORDER) - 1:
             early.advance()
-        if k < len(SMALL_ORDER):
-            late.advance()
+    finish[2]()
     for copy in stores:
         copy.wait()
     for copy in unsent:
@@ -653,7 +689,6 @@
     dma = pltpu.SemaphoreType.DMA
     slots = 2 * CAP
     steps = len(SMALL_ORDER)
-    vmem = pl.BlockSpec(memory_space=pltpu.VMEM)
     anywhere = pl.BlockSpec(memory_space=pl.ANY)
     return pl.pallas_call(
         block_kernel,
@@ -663,13 +698,13 @@
             jax.ShapeDtypeStruct((TILES, TILE_ROWS, LANES), BF16),
             jax.ShapeDtypeStruct((EARLY_ROWS + LATE_ROWS, D), F32),
         ),
-        in_specs=[anywhere if i in (3, 5, 10, 12) else vmem for i in range(len(args))],
-        out_specs=[vmem, vmem, anywhere, vmem],
+        in_specs=[anywhere] * len(args),
+        out_specs=[anywhere] * 4,
         scratch_shapes=[
-            bf(QKV, D),
-            bf(HEADS * HD, D),
-            bf(EXPERTS, D, FF),
-            bf(EXPERTS, FF, D),
+            *(pltpu.VMEM(arg.shape, arg.dtype) for arg in args),
+            bf(ROWS, D),
+            bf(ROWS, D),
+            fl(EARLY_ROWS + LATE_ROWS, D),
             bf(TILES, TILE_ROWS, LANES),
             bf(LANDING, TILE_ROWS, LANES),
             bf(TILES, TILE_ROWS, LANES),
@@ -684,6 +719,10 @@
             bf(2, ROWS, D),
             bf(2, ROWS, D),
             bf(2, ROWS, D),
+            bf(2, ROWS, D),
+            bf(2, ROWS, D),
+            bf(2, ROWS, D),
+            fl(2, 8, ROWS),
             fl(2, 8, ROWS),
             bf(2, ROWS, D),
             bf(2, HEADS, ROWS, HD),
@@ -700,20 +739,22 @@
             bf(EXPERTS, slots, D),
             bf(EXPERTS, slots, D),
             fl(ROWS, D),
+            fl(2, ROWS, D),
             fl(ROWS, D),
             fl(ROWS, D),
             fl(2, ROWS, D),
             fl(2, 2, ROWS),
-            dma((9,)),
-            dma((9,)),
+            dma((10,)),
+            dma((10,)),
             dma((CHAIN_COUNT, PHASES, RING - 1)),
             dma((CHAIN_COUNT, PHASES, RING - 1)),
             dma((CHAIN_COUNT, PHASES - 1, RING - 1)),
             dma((CHAIN_COUNT, PHASES - 1, RING - 1)),
             dma((2, steps, RING - 1)),
             dma((2, steps, RING - 1)),
-            dma((4,)),
             dma((CHAIN_COUNT,)),
+            dma((len(args),)),
+            dma((3,)),
         ],
         compiler_params=pltpu.CompilerParams(
             collective_id=0, has_side_effects=True, vmem_limit_bytes=56 * 1024 * 1024
@@ -721,34 +762,18 @@
     )(*args)
 
 
-def unpack_kernel(
-    block_ref,
-    grad_tok_ref,
-    sum_ref,
-    small_ref,
-    block_out,
-    grad_tok_out,
-    attn_gain,
-    attn_shift,
-    w_qkv_out,
-    qv_bias,
-    w_out_out,
-    out_bias,
-    moe_gain,
-    moe_shift,
-    router,
-    w_in_out,
-    in_bias,
-    w_exp_out,
-    exp_bias,
-    sums,
-    w_qkv,
-    w_out,
-    w_in,
-    w_exp,
-    in_sem,
-    out_sem,
-):
+WIDE = (4, 6, 11, 13)
+
+
+def unpack_kernel(*refs):
+    sources, outs, held = refs[:4], refs[4:19], refs[19:38]
+    in_sem, out_sem, rest_in, rest_out = refs[38:]
+    block_ref, grad_tok_ref, sums, small_ref = held[:4]
+    results = held[4:]
+    block, grad_tok, attn_gain, attn_shift, w_qkv, qv_bias, w_out = results[:7]
+    out_bias, moe_gain, moe_shift, router, w_in, in_bias, w_exp, exp_bias = results[7:]
+    sum_ref = sources[2]
+    w_qkv_out, w_out_out, w_in_out, w_exp_out = (outs[i] for i in WIDE)
     pieces = []
     for e in range(EXPERTS):
         at = e * (IN_TILES + EXP_TILES)
@@ -762,31 +787,42 @@
         rows = pl.ds(at, tiles)
         arriving.append(pltpu.make_async_copy(sum_ref.at[rows], sums.at[rows], in_sem.at[i]))
         arriving[-1].start()
-    block_out[0] = block_ref[:SEQ]
-    grad_tok_out[0] = grad_tok_ref[:SEQ]
+    narrow = [
+        pltpu.make_async_copy(sources[i], held[i], rest_in.at[i]) for i in (0, 1, 3)
+    ]
+    for copy in narrow:
+        copy.start()
+    for copy in narrow:
+        copy.wait()
+    block[0] = block_ref[:SEQ]
+    grad_tok[0] = grad_tok_ref[:SEQ]
     small = small_ref[...]
-    rows = (24, 25, 0, 1, 2)
+    rows = (16, 17, 0, 1, 2)
     for ref, row in zip((attn_gain, attn_shift, out_bias, moe_gain, moe_shift), rows):
         ref[...] = small[row]
     router[...] = small[3:6]
     exp_bias[...] = small[6:9]
     for e in range(EXPERTS):
         for j in range(FF // D):
-            in_bias[e : e + 1, j * D : (j + 1) * D] = small[16 + 2 * e + j : 17 + 2 * e + j]
-    bias = jnp.concatenate([small[32:33], small[33:34]], axis=1)
+            in_bias[e : e + 1, j * D : (j + 1) * D] = small[9 + 2 * e + j : 10 + 2 * e + j]
+    bias = jnp.concatenate([small[18:19], small[19:20]], axis=1)
     for h in range(HEADS):
         at = 3 * h * HD
         qv_bias[h : h + 1, :HD] = bias[:, at : at + HD]
         qv_bias[h : h + 1, HD:] = bias[:, at + 2 * HD : at + 3 * HD]
     leaving = []
-    for i, (at, tiles, rows, lanes, held, out) in enumerate(pieces):
+    for i in range(len(outs)):
+        if i not in WIDE:
+            leaving.append(pltpu.make_async_copy(results[i], outs[i], rest_out.at[i]))
+            leaving[-1].start()
+    for i, (at, tiles, rows, lanes, piece, out) in enumerate(pieces):
         arriving[i].wait()
         per = rows // TILE_ROWS
         for j in range(-(-lanes // LANES)):
             width = min(LANES, lanes - j * LANES)
             part = sums[at + j * per : at + (j + 1) * per].reshape(rows, LANES)
-            held[:, j * LANES : j * LANES + width] = part[:, :width].astype(F32)
-        leaving.append(pltpu.make_async_copy(held, out, out_sem.at[i]))
+            piece[:, j * LANES : j * LANES + width] = part[:, :width].astype(F32)
+        leaving.append(pltpu.make_async_copy(piece, out, out_sem.at[i]))
         leaving[-1].start()
     for copy in leaving:
         copy.wait()
@@ -796,9 +832,7 @@
     def out(shape, dtype=F32):
         return jax.ShapeDtypeStruct(shape, dtype)
 
-    vmem = pl.BlockSpec(memory_space=pltpu.VMEM)
     anywhere = pl.BlockSpec(memory_space=pl.ANY)
-    wide = (4, 6, 11, 13)
     shapes = (
         out((1, SEQ, D), BF16),
         out((1, SEQ, D), BF16),
@@ -819,16 +853,14 @@
     return pl.pallas_call(
         unpack_kernel,
         out_shape=shapes,
-        in_specs=[vmem, vmem, anywhere, vmem],
-        out_specs=[anywhere if i in wide else vmem for i in range(len(shapes))],
+        in_specs=[anywhere] * 4,
+        out_specs=[anywhere] * len(shapes),
         scratch_shapes=[
-            pltpu.VMEM((TILES, TILE_ROWS, LANES), BF16),
-            pltpu.VMEM((QKV, D), F32),
-            pltpu.VMEM((HEADS * HD, D), F32),
-            pltpu.VMEM((EXPERTS, D, FF), F32),
-            pltpu.VMEM((EXPERTS, FF, D), F32),
+            *(pltpu.VMEM(leaf.shape, leaf.dtype) for leaf in args + shapes),
             pltpu.SemaphoreType.DMA((8,)),
             pltpu.SemaphoreType.DMA((8,)),
+            pltpu.SemaphoreType.DMA((4,)),
+            pltpu.SemaphoreType.DMA((len(shapes),)),
         ],
         compiler_params=pltpu.CompilerParams(vmem_limit_bytes=58 * 1024 * 1024),
     )(*args)

time: 95.4 us -> 89.7 us (0.940)
  Pallas kernels: 94.4 us -> 88.8 us
    pallas_call x1, Pallas kernels: 88.2 us -> 83 us  [run_block(): pl.pallas_call(block_kernel, out_shape=(jax.ShapeDtypeStruct((ROWS, D), B...]
where the time goes in v4:
time: 89.7 us
  Pallas kernels  88.8 us (99%)
    pallas_call x1, Pallas kernels, run_block(): pl.pallas_call(block_kernel, out_shape=(jax.ShapeDtypeStruct((ROWS, D), B...  83 us
    pallas_call x1, Pallas kernels, unpack(): pl.pallas_call(unpack_kernel, out_shape=shapes, in_specs=[anywhere] * 4,...  5.88 us

profile of v4, /device:TPU:1, one launch (start us, length us, event | category | flops | bytes accessed | tf_op | source)
XLA Modules:
  0.0 89.7 jit_solution(13899467245176831450)
XLA Ops:
  0.7 83.0 %shard_map.271 = (bf16[208,384]{1,0:T(8,128)(2,1)}, bf16[208,384]{1,0:T(8,128)(2,1)}, bf16[1024,16,128]{2,1,0:T(8,128)(2,1)}, f32[24,384]{1,0:T(8,128)}) custom-call(bf16[1,197,384]{2,1,0:T(8,128)(2,1)} %refs_0_.1, f32[384]{0:T(512)} %refs_1_.1, f32[384]{0:T(512)} %refs_2_.1, bf16[576,384]{1,0:T(8,128)(2,1)} %bitcast.11, bf16[3,128]{1,0:T(4,128)(2,1)} %refs_4_.1, ...), custom_call_target="tpu_custom_call" | custom-call | tf_op jit(solution)/shard_map/pallas_call | solution.py:693
  83.6 5.9 %shard_map.272 = (bf16[1,197,384]{2,1,0:T(8,128)(2,1)}, bf16[1,197,384]{2,1,0:T(8,128)(2,1)}, f32[384]{0:T(512)}, f32[384]{0:T(512)}, f32[576,384]{1,0:T(8,128)}...) custom-call(bf16[208,384]{1,0:T(8,128)(2,1)} %get-tuple-element.34.r, ...), custom_call_target="tpu_custom_call" | custom-call | tf_op jit(solution)/shard_map/pallas_call | solution.py:853

commit v5 on v4

--- a/solution.py
+++ b/solution.py
@@ -20,7 +20,9 @@
 MOE_TILES = EXPERTS * (IN_TILES + EXP_TILES)
 QKV_TILES = (QKV // TILE_ROWS) * (D // LANES)
 OUT_TILES = (HEADS * HD // TILE_ROWS) * (D // LANES)
-BATCHES = ((128, 160),) * EXPERTS + ((64, 96),)
+EXPERT_BATCHES = ((128, 160), (288, 288))
+BATCHES = EXPERT_BATCHES + ((64, 96),)
+READY = (0, None, 1)
 CHAIN_COUNT = 2 * len(BATCHES)
 TILES = sum(sum(batch) for batch in BATCHES)
 ORDERS = (("core", "x", "y", "z"), ("core", "y", "x", "z"))
@@ -558,7 +560,8 @@
         bias = column_sum(gpre_all[e].astype(F32))
         for j in range(FF // D):
             early_held[0, 9 + 2 * e + j : 10 + 2 * e + j] = bias[:, j * D : (j + 1) * D]
-        send_batch(e)
+        if READY[e] is not None:
+            send_batch(READY[e])
 
     def combine(i, ref):
         total = jnp.zeros((ROWS, D), F32)
@@ -577,8 +580,8 @@
         gmoe_copies.append(exchange(6 + i, gmoe_part.at[i], gmoe_other.at[1 - i]))
     mix_part[0] = combine(1, scaled_all).astype(BF16)
     mix_copy = exchange(8, mix_part.at[0], mix_part.at[1])
-    for e in range(EXPERTS):
-        advance_batch(e)
+    for b in range(len(EXPERT_BATCHES)):
+        advance_batch(b)
 
     own_mix = combine(0, scaled_all).astype(BF16).astype(F32)
     bias_rows = jnp.concatenate(
@@ -637,13 +640,13 @@
             held[spot : spot + HD // TILE_ROWS] = tiles.reshape(HD // TILE_ROWS, TILE_ROWS, LANES)
     at += OUT_TILES
     held[at:TILES] = jnp.zeros((TILES - at, TILE_ROWS, LANES), BF16)
-    send_batch(EXPERTS)
+    send_batch(len(EXPERT_BATCHES))
     late_held[0] = jnp.zeros((LATE_ROWS, D), F32)
     bias = column_sum(both.astype(F32))
     late_held[0, 2:3] = bias[:, :D]
     late_held[0, 3:4, 0 : QKV - D] = bias[:, D:]
-    for e in range(EXPERTS):
-        advance_batch(e)
+    for b in range(len(EXPERT_BATCHES)):
+        advance_batch(b)
     early.advance()
     mix_copy.wait_recv()
     block_ref[...] = (
@@ -664,12 +667,12 @@
     finish[1]()
 
     for k in range(2 * PHASES - 1):
-        advance_batch(EXPERTS)
-        if k < 2 * PHASES - 3:
-            for e in range(EXPERTS):
-                advance_batch(e)
+        advance_batch(len(EXPERT_BATCHES))
         if k < len(SMALL_ORDER):
             late.advance()
+        if k < 2 * PHASES - 3:
+            for b in range(len(EXPERT_BATCHES)):
+                advance_batch(b)
         if k < len(SMALL_ORDER) - 1:
             early.advance()
     finish[2]()

time: 89.7 us -> 88.7 us (0.989)
  Pallas kernels: 88.8 us -> 87.8 us
    pallas_call x1, Pallas kernels: 83 us -> 82 us  [run_block(): pl.pallas_call(block_kernel, out_shape=(jax.ShapeDtypeStruct((ROWS, D), B...]
where the time goes in v5:
time: 88.7 us
  Pallas kernels  87.8 us (99%)
    pallas_call x1, Pallas kernels, run_block(): pl.pallas_call(block_kernel, out_shape=(jax.ShapeDtypeStruct((ROWS, D), B...  82 us
    pallas_call x1, Pallas kernels, unpack(): pl.pallas_call(unpack_kernel, out_shape=shapes, in_specs=[anywhere] * 4,...  5.88 us

profile of v5, /device:TPU:1, one launch (start us, length us, event | category | flops | bytes accessed | tf_op | source)
XLA Modules:
  0.0 88.7 jit_solution(1539568936013360052)
XLA Ops:
  0.7 82.0 %shard_map.271 = (bf16[208,384]{1,0:T(8,128)(2,1)}, bf16[208,384]{1,0:T(8,128)(2,1)}, bf16[1024,16,128]{2,1,0:T(8,128)(2,1)}, f32[24,384]{1,0:T(8,128)}) custom-call(bf16[1,197,384]{2,1,0:T(8,128)(2,1)} %refs_0_.1, f32[384]{0:T(512)} %refs_1_.1, f32[384]{0:T(512)} %refs_2_.1, bf16[576,384]{1,0:T(8,128)(2,1)} %bitcast.11, bf16[3,128]{1,0:T(4,128)(2,1)} %refs_4_.1, ...), custom_call_target="tpu_custom_call" | custom-call | tf_op jit(solution)/shard_map/pallas_call | solution.py:696
  82.6 5.9 %shard_map.272 = (bf16[1,197,384]{2,1,0:T(8,128)(2,1)}, bf16[1,197,384]{2,1,0:T(8,128)(2,1)}, f32[384]{0:T(512)}, f32[384]{0:T(512)}, f32[576,384]{1,0:T(8,128)}...) custom-call(bf16[208,384]{1,0:T(8,128)(2,1)} %get-tuple-element.34.r, ...), custom_call_target="tpu_custom_call" | custom-call | tf_op jit(solution)/shard_map/pallas_call | solution.py:856
